TPU v7x, 128 devices: a whole 4x4x4 slice. The times are simulated.
128 devices in a mesh: node: 32 (over z, y, core), rep: 4 (over x).
Axes of the slice: x: 4, y: 4, z: 4, core: 2. Of those that a mesh axis runs over, the one named last changes fastest.
Arguments:
- embeddings: bfloat16 [262144, 512], P(('node', 'rep')), may hold values from -6 to 6
- w_first: bfloat16 [512, 512], replicated, may hold values from -0.25 to 0.25
- w_second: bfloat16 [512, 512], replicated, may hold values from -0.25 to 0.25
- w_score: bfloat16 [512], replicated, may hold values from -0.5 to 0.5
- src_row: int32 [65536], P(('node', 'rep')), may hold values from 0 to 2047
- dst_owner: int32 [65536, 1], P(('node', 'rep')), may hold values from 0 to 127; in each aligned block of 512 rows (0 to 511, 512 to 1023, ...) at most 8 rows name the same one
- dst_row: int32 [65536], P(('node', 'rep')), may hold values from 0 to 2047
- edge_count: int32 [128], replicated, may hold values from 1 to 512, as said below
- neg_ids: int32 [8], replicated, may hold values from 0 to 262143
Outputs:
- grad_embeddings: float32 [262144, 512], P(('node', 'rep'))
- grad_first: float32 [512, 512], replicated
- grad_second: float32 [512, 512], replicated
- grad_score: float32 [512], replicated
- loss: float32 [], replicated
Inputs may be any that keep to these rules, and one draw needn't show every extreme that they name: `dst_owner`: among the 512 slots of one device no owner is named more than 8 times, a bound that some block reaches. `edge_count`: some device has all 512 slots live.
All inputs are finite; a program needn't handle non-finite values.
Results may differ from a plain program's by a relative error of at most 0.0035.
Values may be sent and summed in bfloat16 or wider, within the bound.
No kernel may reach another device: no remote copies, remote signals or barrier semaphores. Data moves between devices by JAX's collectives and lax.ppermute only.
A program may use at most 128 MiB of HBM per device.

v0:
```python
import jax
import jax.numpy as jnp
from jax import lax
from jax.sharding import PartitionSpec as P


def silu_slope(value):
    sig = jax.nn.sigmoid(value)
    return sig * (1.0 + value * (1.0 - sig))


def decode(src_emb, dst_emb, negatives, w_first, w_second, w_score, live, total):
    edges = src_emb.shape[0]
    width = src_emb.shape[1]
    count_neg = negatives.shape[0]
    src_f = src_emb.astype(jnp.float32)
    dst_f = dst_emb.astype(jnp.float32)
    neg_f = negatives.astype(jnp.float32)
    x_pos = (src_f * dst_f).astype(jnp.bfloat16)
    x_neg = (
        (src_f[:, None, :] * neg_f[None, :, :])
        .reshape(edges * count_neg, width)
        .astype(jnp.bfloat16)
    )
    stacked = jnp.concatenate([x_pos, x_neg], axis=0)
    z_one = jnp.dot(stacked, w_first, preferred_element_type=jnp.float32)
    a_one = jax.nn.silu(z_one).astype(jnp.bfloat16)
    z_two = jnp.dot(a_one, w_second, preferred_element_type=jnp.float32)
    a_two = jax.nn.silu(z_two).astype(jnp.bfloat16)
    score = jnp.dot(a_two, w_score, preferred_element_type=jnp.float32)
    pos_score = score[:edges]
    neg_score = score[edges:].reshape(edges, count_neg)
    loss = (
        jnp.sum(live * jax.nn.softplus(-pos_score))
        + jnp.sum(live[:, None] * jax.nn.softplus(neg_score)) / count_neg
    ) / total
    ds_pos = -jax.nn.sigmoid(-pos_score) * live / total
    ds_neg = jax.nn.sigmoid(neg_score) * live[:, None] / (count_neg * total)
    slope = jnp.concatenate([ds_pos, ds_neg.reshape(-1)], axis=0)
    grad_score = jnp.dot(slope, a_two, preferred_element_type=jnp.float32)
    dz_two = (slope[:, None] * w_score.astype(jnp.float32)[None, :] * silu_slope(z_two)).astype(
        jnp.bfloat16
    )
    grad_second = jnp.dot(a_one.T, dz_two, preferred_element_type=jnp.float32)
    dz_one = (
        jnp.dot(dz_two, w_second.T, preferred_element_type=jnp.float32) * silu_slope(z_one)
    ).astype(jnp.bfloat16)
    grad_first = jnp.dot(stacked.T, dz_one, preferred_element_type=jnp.float32)
    d_input = jnp.dot(dz_one, w_first.T, preferred_element_type=jnp.float32)
    dx_pos = d_input[:edges]
    dx_neg = d_input[edges:].reshape(edges, count_neg, width)
    grad_src = dx_pos * dst_f + jnp.einsum("ekd,kd->ed", dx_neg, neg_f)
    grad_dst = dx_pos * src_f
    grad_neg = jnp.einsum("ekd,ed->kd", dx_neg, src_f)
    return (grad_src, grad_dst, grad_neg, grad_first, grad_second, grad_score, loss)


def ask_owners(requests):
    return lax.all_to_all(requests, ("node", "rep"), split_axis=0, concat_axis=0, tiled=True)


def serve_rows(served):
    return lax.all_to_all(served, ("node", "rep"), split_axis=0, concat_axis=0, tiled=True)


def return_grads(slot_grads):
    return lax.all_to_all(slot_grads, ("node", "rep"), split_axis=0, concat_axis=0, tiled=True)


def body(embeddings, w_first, w_second, w_score, src_row, dst_owner, dst_row, edge_count, neg_ids):
    devices = lax.axis_size(("node", "rep"))
    me_index = lax.axis_index(("node", "rep"))
    own_rows = embeddings.shape[0]
    width = embeddings.shape[1]
    edges = src_row.shape[0]
    capacity = max(2, 2 * edges // devices)
    total = jnp.sum(edge_count).astype(jnp.float32)
    live = (jnp.arange(edges, dtype=jnp.int32) < edge_count[me_index]).astype(jnp.float32)
    owners = dst_owner[:, 0]
    onehot = (owners[:, None] == jnp.arange(devices, dtype=jnp.int32)[None, :]).astype(jnp.int32)
    ranks = jnp.sum(jnp.cumsum(onehot, axis=0) * onehot, axis=1) - 1
    position = owners * capacity + ranks
    requests = (
        jnp.zeros((devices * capacity,), jnp.int32)
        .at[position]
        .set(dst_row)
        .reshape(devices, capacity)
    )
    wanted = ask_owners(requests)
    neg_local = neg_ids % own_rows
    neg_mine = neg_ids // own_rows == me_index
    offered = jnp.where(neg_mine[:, None], embeddings[neg_local].astype(jnp.float32), 0.0)
    negatives = lax.psum(offered, ("node", "rep")).astype(jnp.bfloat16)
    served = embeddings[wanted]
    fetched = serve_rows(served)
    dst_emb = fetched.reshape(devices * capacity, width)[position]
    src_emb = embeddings[src_row]
    grad_src, grad_dst, grad_neg, grad_first, grad_second, grad_score, loss = decode(
        src_emb, dst_emb, negatives, w_first, w_second, w_score, live, total
    )
    slot_grads = jnp.zeros((devices * capacity, width), jnp.float32).at[position].set(grad_dst)
    arrived = return_grads(slot_grads.reshape(devices, capacity, width))
    grads = jnp.zeros((own_rows, width), jnp.float32).at[src_row].add(grad_src)
    grads = grads.at[wanted.reshape(-1)].add(arrived.reshape(devices * capacity, width))
    grad_neg, grad_first, grad_second, grad_score, loss = lax.psum(
        (grad_neg, grad_first, grad_second, grad_score, loss), ("node", "rep")
    )
    grads = grads.at[neg_local].add(jnp.where(neg_mine[:, None], grad_neg, 0.0))
    return (grads, grad_first, grad_second, grad_score, loss)


def solution(mesh):
    in_specs = (
        P(("node", "rep"), None),
        P(),
        P(),
        P(),
        P(("node", "rep")),
        P(("node", "rep"), None),
        P(("node", "rep")),
        P(),
        P(),
    )
    out_specs = (P(("node", "rep"), None), P(), P(), P(), P())
    return jax.shard_map(body, mesh=mesh, in_specs=in_specs, out_specs=out_specs, check_vma=False)
```

profile of v0, /device:TPU:1, one launch (start us, length us, event | category | flops | bytes accessed | tf_op | source)
XLA Modules:
  0.0 357.7 jit_solution(2757760582443301742)
XLA Ops:
  7.2 0.9 copy.20
  8.1 0.2 fusion.20
  8.5 0.9 fusion.19
  9.4 0.7 compare_select_fusion.3
  10.1 2.6 scatter_custom_fusion
  12.7 0.7 all_to_all.14
  13.4 11.5 %all-to-all-start = ((s32[128,1,8]{2,1,0:T(1,128)}), s32[128,1,8]{2,1,0:T(1,128)S(1)}, u32[]{:S(2)}, u32[]{:S(2)}) async-start(s32[128,1,8]{2,1,0:T(1,128)} %bitcast.12), calls=%async_computation | async-start | bytes 131072 | tf_op jit(solution)/shard_map/all_to_all | solution.py:59
  24.9 0.7 fusion.34
  25.6 0.7 compare_select_fusion.6
  26.2 0.7 compare_select_fusion.5
  27.0 0.6 gather_fusion.3
  27.6 67.2 %psum.42 = bf16[8,512]{1,0:T(8,128)(2,1)S(1)} all-reduce(f32[8,512]{1,0:T(8,128)S(1)} %convert_select_fusion), channel_id=1, replica_groups=mesh['node'=32,'rep'=4] {'node','rep'}, use_global_device_ids=true, to_apply=%region_4.5 | all-reduce | flops 4096 | bytes 24576 | tf_op jit(solution)/shard_map/psum | solution.py:93
  94.8 2.0 gather_fusion
  96.8 1.6 bitcast_convert_fusion
  98.4 0.6 dynamic_slice.3
  98.9 0.6 fusion.33
  99.6 0.6 reduce_sum.37
  101.0 5.1 %gather_fusion.1 = bf16[1024,512]{1,0:T(8,128)(2,1)} fusion(bf16[2048,512]{1,0:T(8,128)(2,1)S(1)} %copy-done, s32[1024]{0:T(1024)S(1)} %broadcast_clamp_fusion), kind=kCustom, calls=%fused_computation.1 | custom fusion | bytes 2101248 | tf_op jit(solution)/shard_map/gather | solution.py:94
  106.1 4.7 %all-to-all-start.1 = ((bf16[128,8,512]{2,1,0:T(8,128)(2,1)}), bf16[128,8,512]{2,1,0:T(8,128)(2,1)S(1)}, u32[]{:S(2)}, u32[]{:S(2)}) async-start(bf16[128,8,512]{2,1,0:T(8,128)(2,1)} %bitcast.68), calls=%async_computation.1 | async-start | bytes 2097152 | tf_op jit(solution)/shard_map/all_to_all | solution.py:63
  110.8 4.0 %fusion.2 = bf16[4096,512]{1,0:T(8,128)(2,1)} fusion(f32[8,512]{1,0:T(8,128)S(1)} %get-tuple-element.17, f32[512,512]{1,0:T(8,128)} %get-tuple-element.11), kind=kLoop, calls=%fused_computation.21 | loop fusion | flops 4194304 | bytes 5259264 | tf_op jit(solution)/shard_map/convert_element_type | solution.py:23
  114.8 0.5 broadcast.180
  115.3 0.8 reduce.9
  116.2 14.2 %all-to-all-done.1 = bf16[128,8,512]{2,1,0:T(8,128)(2,1)S(1)} async-done(((bf16[128,8,512]{2,1,0:T(8,128)(2,1)}), bf16[128,8,512]{2,1,0:T(8,128)(2,1)S(1)}, u32[]{:S(2)}, u32[]{:S(2)}) %all-to-all-start.1) | async-done | bytes 1048608 | tf_op jit(solution)/shard_map/all_to_all | solution.py:63
  130.4 2.0 gather_fusion.2
  132.5 8.1 %multiply_convert_fusion.3 = (bf16[4608,512]{1,0:T(8,128)(2,1)S(1)}, f32[4608,512]{1,0:T(8,128)}) fusion(bf16[512,512]{1,0:T(8,128)(2,1)S(1)} %copy-done.6, bf16[4096,512]{1,0:T(8,128)(2,1)} %fusion.2, bf16[512,512]{1,0:T(8,128)(2,1)S(1)} %fusion.9), kind=kOutput, calls=%fused_computation.13 | convolution fusion | flops 2437152768 | bytes 19398656 | tf_op jit(solution)/shard_map/dot_general | solution.py:26
  140.6 6.4 %multiply_convert_fusion.2 = (bf16[4608,512]{1,0:T(8,128)(2,1)S(1)}, f32[4608,512]{1,0:T(8,128)}) fusion(bf16[4608,512]{1,0:T(8,128)(2,1)S(1)} %get-tuple-element.18, bf16[512,512]{1,0:T(8,128)(2,1)S(1)} %copy-done.8), kind=kOutput, calls=%fused_computation.11 | convolution fusion | flops 2427715584 | bytes 19398656 | tf_op jit(solution)/shard_map/dot_general | solution.py:28
  147.0 2.1 copy-done.2
  149.1 1.3 convolution_reduce_fusion
  150.5 1.3 fusion.30
  151.7 0.2 slice.32
  152.0 0.6 fusion.24
  152.9 7.3 %multiply_convert_fusion.1 = bf16[4608,512]{1,0:T(8,128)(2,1)S(1)} fusion(f32[4608,512]{1,0:T(8,128)} %get-tuple-element.21, f32[512]{0:T(512)S(1)} %convert_element_type.71, f32[4608]{0:T(1024)S(1)} %pad_maximum_fusion.3), kind=kLoop, calls=%fused_computation.10 | loop fusion | flops 23592960 | bytes 14176256 | tf_op jit(solution)/shard_map/convert_element_type | solution.py:41
  160.3 4.2 %multiply_convert_fusion = bf16[4608,512]{1,0:T(8,128)(2,1)S(1)} fusion(f32[4608,512]{1,0:T(8,128)S(1)} %copy-done.12, bf16[4608,512]{1,0:T(8,128)(2,1)S(1)} %multiply_convert_fusion.1, bf16[512,512]{1,0:T(8,128)(2,1)S(1)} %copy-done.9), kind=kOutput, calls=%fused_computation.9 | convolution fusion | flops 2437152768 | bytes 19398656 | tf_op jit(solution)/shard_map/dot_general | solution.py:46
  164.5 3.6 %fusion.3 = f32[512,512]{1,0:T(8,128)} fusion(bf16[4608,512]{1,0:T(8,128)(2,1)S(1)} %multiply_convert_fusion, bf16[4096,512]{1,0:T(8,128)(2,1)S(1)} %copy-done.4, bf16[512,512]{1,0:T(8,128)(2,1)S(1)} %fusion.9), kind=kOutput, calls=%fused_computation.22 | convolution fusion | flops 2425356288 | bytes 10485760 | tf_op jit(solution)/shard_map/dot_general | solution.py:48
  168.1 5.2 %fusion.37 = f32[4608,512]{1,0:T(8,128)} fusion(bf16[4608,512]{1,0:T(8,128)(2,1)S(1)} %multiply_convert_fusion, bf16[512,512]{1,0:T(8,128)(2,1)S(1)} %copy-done.6), kind=kOutput, calls=%fused_computation.88 | convolution fusion | flops 2415919104 | bytes 14680064 | tf_op jit(solution)/shard_map/dot_general | solution.py:49
  173.3 4.4 %scatter_custom_fusion.2 = f32[1024,512]{1,0:T(8,128)} fusion(s32[512]{0:T(512)S(1)} %bitcast.79, f32[]{:T(128)} %constant.34.clone.1, f32[4608,512]{1,0:T(8,128)} %fusion.37, bf16[512,512]{1,0:T(8,128)(2,1)S(1)} %gather_fusion), kind=kCustom, calls=%fused_computation.34 | custom fusion | flops 524288 | bytes 3670528 | tf_op jit(solution)/shard_map/scatter | solution.py:101
  177.7 4.9 %all-to-all-start.2 = ((f32[128,8,512]{2,1,0:T(8,128)}), f32[128,8,512]{2,1,0:T(8,128)}, u32[]{:S(2)}, u32[]{:S(2)}) async-start(f32[128,8,512]{2,1,0:T(8,128)} %bitcast.21), calls=%async_computation.2 | async-start | bytes 4194304 | tf_op jit(solution)/shard_map/all_to_all | solution.py:67
  182.6 7.4 %fusion.38 = f32[512,512]{1,0:T(8,128)} fusion(bf16[4608,512]{1,0:T(8,128)(2,1)} %copy-done.11, bf16[4608,512]{1,0:T(8,128)(2,1)} %copy-done.3), kind=kOutput, calls=%fused_computation.89 | convolution fusion | flops 2415919104 | bytes 10485760 | tf_op jit(solution)/shard_map/dot_general | solution.py:44
  190.1 6.4 %fusion.1 = f32[512,512]{0,1:T(8,128)S(1)} fusion(f32[4608,512]{1,0:T(8,128)} %fusion.37, f32[512,8]{0,1:T(8,128)S(1)} %get-tuple-element.16), kind=kLoop, calls=%fused_computation.18 | loop fusion | flops 3932160 | bytes 9453568 | tf_op jit(solution)/shard_map/ekd,kd->ed/dot_general | solution.py:52
  197.8 6.9 %scatter_custom_fusion.1 = f32[2048,512]{1,0:T(8,128)} fusion(s32[512]{0:T(512)S(1)} %compare_select_fusion.5, f32[]{:T(128)} %constant.34.clone.1, bf16[512,512]{1,0:T(8,128)(2,1)S(1)} %gather_fusion.2, f32[512,512]{0,1:T(8,128)S(1)} %fusion.1, f32[4608,512]{1,0:T(8,128)} %fusion.37), kind=kCustom, calls=%fused_computation.26 | custom fusion | flops 1048576 | bytes 6816256 | tf_op jit(solution)/shard_map/scatter-add | solution.py:103
  204.7 3.1 fusion.39
  207.8 4.3 %fusion = f32[512,8]{0,1:T(8,128)S(1)} fusion(f32[4608,512]{1,0:T(8,128)} %fusion.37, f32[512,512]{0,1:T(8,128)S(1)} %copy-done.5), kind=kLoop, calls=%fused_computation.16 | loop fusion | flops 4190208 | bytes 9453568 | tf_op jit(solution)/shard_map/ekd,ed->kd/dot_general | solution.py:54
  212.1 68.0 %all-reduce = (f32[8,512]{1,0:T(8,128)S(1)}, f32[512]{0:T(512)}, f32[]{:T(128)}) all-reduce(f32[8,512]{1,0:T(8,128)S(1)} %bitcast.72, f32[512]{0:T(512)S(1)} %bitcast.76, f32[]{:T(128)S(6)} %div.58), channel_id=1, replica_groups=mesh['node'=32,'rep'=4] {'node','rep'}, use_global_device_ids=true, to_apply=%region_9.10 | all-reduce | flops 4609 | bytes 36872 | tf_op jit(solution)/shard_map/psum | solution.py:105
  280.1 11.7 %scatter_custom_fusion.3 = f32[2048,512]{1,0:T(8,128)} fusion(f32[2048,512]{1,0:T(8,128)} %scatter_custom_fusion.1, s32[1024]{0:T(1024)S(1)} %bitcast.81, f32[128,8,512]{2,1,0:T(8,128)} %all-to-all-done.2), kind=kCustom, calls=%fused_computation.24 | custom fusion | flops 524288 | bytes 6291456 | tf_op jit(solution)/shard_map/scatter-add | solution.py:104
  291.8 4.9 %scatter_custom_fusion.4 = f32[2048,512]{1,0:T(8,128)} fusion(f32[2048,512]{1,0:T(8,128)} %scatter_custom_fusion.3, s32[8]{0:T(128)S(1)} %compare_select_fusion.6, f32[8,512]{1,0:T(8,128)S(1)} %get-tuple-element.5, f32[]{:T(128)} %constant.34.clone.1, pred[8]{0:T(512)(128)(4,1)S(1)} %fusion.34), kind=kCustom, calls=%fused_computation.55 | custom fusion | flops 8192 | bytes 4211712 | tf_op jit(solution)/shard_map/scatter-add | solution.py:108
  296.7 49.6 %all-reduce.4.cloned.1.call-done = (f32[512,512]{1,0:T(8,128)}, f32[512,512]{1,0:T(8,128)}) async-done(((f32[512,512]{1,0:T(8,128)}, f32[512,512]{1,0:T(8,128)}), (f32[512,512]{1,0:T(8,128)}, f32[512,512]{1,0:T(8,128)})) %all-reduce.4.cloned.1.call-update) | async-done | bytes 2097168 | tf_op jit(solution)/shard_map/psum | solution.py:105
  346.3 2.3 copy.50
  348.6 2.3 copy.51
  (55 shorter events, 1.1 us)
Async XLA Ops:
  7.2 19.8 %copy-start = (bf16[2048,512]{1,0:T(8,128)(2,1)S(1)}, bf16[2048,512]{1,0:T(8,128)(2,1)}, u32[]{:S(2)}) copy-start(bf16[2048,512]{1,0:T(8,128)(2,1)} %param.9) | copy-start | bytes 6291460
  8.1 90.2 %copy-start.10 = (s32[128]{0:T(128)S(1)}, s32[128]{0:T(128)}, u32[]{:S(2)}) copy-start(s32[128]{0:T(128)} %param.16) | copy-start | bytes 1540
  8.1 92.1 %copy-start.7 = (bf16[512]{0:T(512)(128)(2,1)S(1)}, bf16[512]{0:T(512)(128)(2,1)}, u32[]{:S(2)}) copy-start(bf16[512]{0:T(512)(128)(2,1)} %param.12) | copy-start | bytes 3076
  13.4 87.5 %all-to-all-start = ((s32[128,1,8]{2,1,0:T(1,128)}), s32[128,1,8]{2,1,0:T(1,128)S(1)}, u32[]{:S(2)}, u32[]{:S(2)}) async-start(s32[128,1,8]{2,1,0:T(1,128)} %bitcast.12), calls=%async_computation | async-start | bytes 131072 | tf_op jit(solution)/shard_map/all_to_all | solution.py:59
  106.1 24.3 %all-to-all-start.1 = ((bf16[128,8,512]{2,1,0:T(8,128)(2,1)}), bf16[128,8,512]{2,1,0:T(8,128)(2,1)S(1)}, u32[]{:S(2)}, u32[]{:S(2)}) async-start(bf16[128,8,512]{2,1,0:T(8,128)(2,1)} %bitcast.68), calls=%async_computation.1 | async-start | bytes 2097152 | tf_op jit(solution)/shard_map/all_to_all | solution.py:63
  110.8 21.7 %copy-start.6 = (bf16[512,512]{1,0:T(8,128)(2,1)S(1)}, bf16[512,512]{1,0:T(8,128)(2,1)}, u32[]{:S(2)}) copy-start(bf16[512,512]{1,0:T(8,128)(2,1)} %param.10) | copy-start | bytes 1572868
  132.5 8.1 %copy-start.8 = (bf16[512,512]{1,0:T(8,128)(2,1)S(1)}, bf16[512,512]{1,0:T(8,128)(2,1)}, u32[]{:S(2)}) copy-start(bf16[512,512]{1,0:T(8,128)(2,1)} %param.11) | copy-start | bytes 1572868
  140.6 6.4 %copy-start.11 = (bf16[4608,512]{1,0:T(8,128)(2,1)}, bf16[4608,512]{1,0:T(8,128)(2,1)S(1)}, u32[]{:S(2)}) copy-start(bf16[4608,512]{1,0:T(8,128)(2,1)S(1)} %get-tuple-element.18) | copy-start | bytes 14155780
  147.0 2.1 copy-start.2
  152.9 7.4 %copy-start.9 = (bf16[512,512]{1,0:T(8,128)(2,1)S(1)}, bf16[512,512]{1,0:T(8,128)(2,1)}, u32[]{:S(2)}) copy-start(bf16[512,512]{1,0:T(8,128)(2,1)} %param.11) | copy-start | bytes 1572868
  152.9 7.4 %copy-start.12 = (f32[4608,512]{1,0:T(8,128)S(1)}, f32[4608,512]{1,0:T(8,128)}, u32[]{:S(2)}) copy-start(f32[4608,512]{1,0:T(8,128)} %get-tuple-element.19) | copy-start | bytes 28311556
  160.3 4.2 %copy-start.3 = (bf16[4608,512]{1,0:T(8,128)(2,1)}, bf16[4608,512]{1,0:T(8,128)(2,1)S(1)}, u32[]{:S(2)}) copy-start(bf16[4608,512]{1,0:T(8,128)(2,1)S(1)} %multiply_convert_fusion.1) | copy-start | bytes 14155780
  160.3 4.2 %copy-start.4 = (bf16[4096,512]{1,0:T(8,128)(2,1)S(1)}, bf16[4096,512]{1,0:T(8,128)(2,1)}, u32[]{:S(2)}) copy-start(bf16[4096,512]{1,0:T(8,128)(2,1)} %fusion.2) | copy-start | bytes 12582916
  177.7 102.5 %all-to-all-start.2 = ((f32[128,8,512]{2,1,0:T(8,128)}), f32[128,8,512]{2,1,0:T(8,128)}, u32[]{:S(2)}, u32[]{:S(2)}) async-start(f32[128,8,512]{2,1,0:T(8,128)} %bitcast.21), calls=%async_computation.2 | async-start | bytes 4194304 | tf_op jit(solution)/shard_map/all_to_all | solution.py:67
  182.6 163.7 %all-reduce.4.cloned.1.call-start = ((), (), s32[]{:S(2)}) async-start(), calls=%async_computation.3 | async-start | bytes 4194304 | tf_op jit(solution)/shard_map/psum | solution.py:105
  197.8 10.0 %copy-start.5 = (f32[512,512]{0,1:T(8,128)S(1)}, f32[512,512]{0,1:T(8,128)}, u32[]{:S(2)}) copy-start(f32[512,512]{0,1:T(8,128)} %get-tuple-element.10) | copy-start | bytes 3145732
  280.1 70.7 %copy-start.1 = (bf16[2048,512]{1,0:T(8,128)(2,1)S(1)}, bf16[2048,512]{1,0:T(8,128)(2,1)}, u32[]{:S(2)}) copy-start(bf16[2048,512]{1,0:T(8,128)(2,1)} %param.9) | copy-start | bytes 6291460
Sparse Core Ops, SparseCore 0:
  190.2 156.0 all-reduce.3
where the time goes:
time: 359 us; the launch traced here: 358 us
  blocking collectives  135 us (38%)
  waiting for transfers between devices  63.8 us (18%)
  other arithmetic  59.6 us (17%)
  matrix products  39.2 us (11%)
  local copies, waits for them, and re-layouts  22.4 us (6%)
  starting transfers between devices  21.1 us (6%)
  between operations  16.4 us (5%)
    psum x1, blocking collectives, body(): lax.psum((grad_neg, grad_first, grad_second, grad_score, loss), ('node',...  68 us
    psum x1, blocking collectives, body(): negatives = lax.psum(offered, ('node', 'rep')).astype(jnp.bfloat16)  67.2 us
    psum x1, waiting for transfers between devices, body(): lax.psum((grad_neg, grad_first, grad_second, grad_score, loss), ('node',...  49.6 us
    all_to_all x1, waiting for transfers between devices, serve_rows(): lax.all_to_all(served, ('node', 'rep'), split_axis=0, concat_axis=0, tile...  14.2 us
    scatter-add x1, other arithmetic, body(): grads.at[wanted.reshape(-1)].add(arrived.reshape(devices * capacity, width))  11.7 us
    all_to_all x1, starting transfers between devices, ask_owners(): lax.all_to_all(requests, ('node', 'rep'), split_axis=0, concat_axis=0, ti...  11.5 us
    dot_general x1, matrix products, decode(): z_one = jnp.dot(stacked, w_first, preferred_element_type=jnp.float32)  8.06 us
    dot_general x1, matrix products, decode(): grad_second = jnp.dot(a_one.T, dz_two, preferred_element_type=jnp.float32)  7.4 us
  transfers between devices with their start and end apart: 4, of which 2 were waited for; matrix products, arithmetic and copies ran while one was open for 16% of the time, Pallas kernels for 0%

commit v1 on v0

v1 whole, which is shorter than its diff:
```python
import jax
import jax.numpy as jnp
from jax import lax
from jax.experimental import pallas as pl
from jax.experimental.pallas import tpu as pltpu
from jax.sharding import Mesh, PartitionSpec as P

F32 = jnp.float32
BF16 = jnp.bfloat16
AXES = ("z", "y", "c", "x")
CHIPS = ("z", "y", "x")
VMEM = pl.BlockSpec(memory_space=pltpu.VMEM)
SMEM = pl.BlockSpec(memory_space=pltpu.SMEM)
HBM = pl.BlockSpec(memory_space=pltpu.HBM)
MIB = 1 << 20


def in_hbm(*arrays):
    return tuple(pltpu.with_memory_space_constraint(a, pltpu.HBM) for a in arrays)


DEVICES = 128
GROUP = 64
ROWS = 2048
EDGES = 512
WIDTH = 512
NEG = 8
CAP = 8
SLOTS = DEVICES * CAP
LANES = 128
WIDE = WIDTH + LANES
TALL = WIDTH + 16


def mm(a, b):
    return jnp.dot(a, b, preferred_element_type=F32)


def mm_nt(a, b):
    return lax.dot_general(a, b, (((1,), (1,)), ((), ())), preferred_element_type=F32)


def mm_tn(a, b):
    return lax.dot_general(a, b, (((0,), (0,)), ((), ())), preferred_element_type=F32)


def wide(value):
    return jnp.concatenate([value] * (WIDTH // LANES), axis=1)


def iota(shape, dim):
    return lax.broadcasted_iota(jnp.int32, shape, dim)


def one(mask):
    return jnp.where(mask, 1.0, 0.0).astype(BF16)


def column(row):
    return jnp.transpose(jnp.broadcast_to(row.astype(F32), (LANES, row.shape[1]))).astype(jnp.int32)


def onehot_rows(col, count):
    lane = iota(col.shape, 1)
    return jnp.concatenate([one(col == lane + LANES * j) for j in range(count // LANES)], axis=1)


def split(value):
    high = value.astype(BF16)
    return high, (value - high.astype(F32)).astype(BF16)


def softplus(value):
    return jnp.maximum(value, 0.0) + jnp.log1p(jnp.exp(-jnp.abs(value)))


def gate(half):
    t = jnp.tanh(half)
    m = half * t
    return half + m, (1.0 + t) * (1.0 + (half - m))


def counts(ec_ref):
    me = lax.axis_index(AXES)
    ec = ec_ref[...]
    mine = jnp.sum(jnp.where(iota(ec.shape, 1) == me, ec, 0).astype(F32), axis=1, keepdims=True)
    return mine, jnp.sum(ec.astype(F32), axis=1, keepdims=True)


def prepare_kernel(emb_hbm, src_hbm, owner_hbm, dst_hbm, ec_hbm, neg_hbm, push_ref, semb_hbm, pos_ref,
                   emb_ref, src_ref, owner_ref, dst_ref, ec_ref, neg_ref, semb_ref, sems):
    pairs = [(neg_hbm, neg_ref), (ec_hbm, ec_ref), (owner_hbm, owner_ref), (src_hbm, src_ref),
             (dst_hbm, dst_ref), (emb_hbm, emb_ref)]
    copies = [pltpu.make_async_copy(a, b, sems.at[i]) for i, (a, b) in enumerate(pairs)]
    for copy in copies:
        copy.start()
    for copy in copies[:-1]:
        copy.wait()
    me = lax.axis_index(AXES)
    mine, _ = counts(ec_ref)
    live = iota((1, EDGES), 1).astype(F32) < mine
    owner = jnp.where(live, owner_ref[...], -1)
    named = one(iota((DEVICES, EDGES), 0) == owner)
    before = one(iota((EDGES, EDGES), 0) < iota((EDGES, EDGES), 1))
    rank = jnp.sum(mm(named, before) * named.astype(F32), axis=0, keepdims=True)
    pos = jnp.where(live, owner * CAP + rank.astype(jnp.int32), -1)
    pos_ref[...] = pos
    row = column(dst_ref[...])
    lane = iota((EDGES, LANES), 1)
    meta = jnp.where(lane == 0, row // 64, jnp.where(lane == 1, row % 64, jnp.where(lane == 2, 1, 0)))
    meta = meta.astype(F32).astype(BF16)
    sub = iota((NEG, LANES), 0)
    local = jnp.zeros((NEG, LANES), jnp.int32)
    for k in range(NEG):
        local = jnp.where(sub == k, neg_ref[k] - me * ROWS, local)
    offered = onehot_rows(local, ROWS)
    chosen = onehot_rows(column(src_ref[...]), ROWS)
    copies[-1].wait()
    emb = emb_ref[...]
    semb = mm(chosen, emb).astype(BF16)
    semb_ref[...] = semb
    out = pltpu.make_async_copy(semb_ref, semb_hbm, sems.at[6])
    out.start()
    offers = mm(offered, emb)
    high = iota((NEG, LANES), 1) >= LANES // 2
    pieces = []
    for q in range(4):
        tile = offers[:, LANES * q:LANES * (q + 1)]
        pieces += [jnp.where(high, pltpu.roll(tile, LANES // 2, 1), 0.0), jnp.where(high, tile, 0.0)]
    pieces = jnp.concatenate(pieces, axis=0)
    count = SLOTS // 4
    for q in range(4):
        rows = pl.ds(q * count, count)
        place = one(iota((count, EDGES), 0) + q * count == pos)
        push_ref[rows, 0:WIDTH] = mm(place, semb).astype(BF16)
        push_ref[rows, WIDTH:] = (mm(place, meta) + jnp.concatenate([pieces] * (count // 64), axis=0)).astype(BF16)
    out.wait()


def prepare(emb, src_row, owner, dst_row, ec, neg_ids):
    return pl.pallas_call(
        prepare_kernel,
        in_specs=[HBM] * 6,
        out_specs=[VMEM, HBM, VMEM],
        out_shape=[
            pltpu.VMEM((SLOTS, WIDE), BF16),
            pltpu.HBM((EDGES, WIDTH), BF16),
            jax.ShapeDtypeStruct((1, EDGES), jnp.int32),
        ],
        scratch_shapes=[
            pltpu.VMEM((ROWS, WIDTH), BF16),
            pltpu.VMEM((1, EDGES), jnp.int32),
            pltpu.VMEM((1, EDGES), jnp.int32),
            pltpu.VMEM((1, EDGES), jnp.int32),
            pltpu.VMEM((1, DEVICES), jnp.int32),
            pltpu.SMEM((NEG,), jnp.int32),
            pltpu.VMEM((EDGES, WIDTH), BF16),
            pltpu.SemaphoreType.DMA((7,)),
        ],
        compiler_params=pltpu.CompilerParams(vmem_limit_bytes=24 * MIB),
        name="prepare",
    )(*in_hbm(emb, src_row, owner, dst_row, ec, neg_ids))


def pick_kernel(recv_ref, out_ref):
    told = recv_ref[:, WIDTH:].astype(F32)
    piece = jnp.sum(told.reshape(DEVICES, CAP, LANES), axis=0)
    part = lax.axis_index("c") * 4 + lax.axis_index("x")
    high = iota((NEG, LANES), 1) >= LANES // 2
    for i in range(4):
        low = jnp.logical_and(jnp.logical_not(high), part == 2 * i)
        tile = jnp.where(low, pltpu.roll(piece, LANES // 2, 1), 0.0)
        tile = jnp.where(jnp.logical_and(high, part == 2 * i + 1), piece, tile)
        out_ref[:, LANES * i:LANES * (i + 1)] = tile


def pick(recv):
    return pl.pallas_call(
        pick_kernel,
        in_specs=[VMEM],
        out_specs=VMEM,
        out_shape=jax.ShapeDtypeStruct((NEG, WIDTH), F32),
        compiler_params=pltpu.CompilerParams(vmem_limit_bytes=16 * MIB),
        name="pick",
    )(recv)


def stack(parts):
    return jnp.concatenate(parts, axis=0) if len(parts) > 1 else parts[0]


def decode_parts(xs, heads, w1, w2, wsb, wsr, g1_ref, g2_ref, ready=None, summed=None):
    first = [gate(mm(x, w1)) for x in xs]
    a1s = [a.astype(BF16) for a, _ in first]
    second = [gate(mm(a, w2)) for a in a1s]
    dz2s = []
    for (a2, slope), head in zip(second, heads):
        ds = wide(head(mm(a2.astype(BF16), wsb), a2))
        dz2s.append((ds * (wsr * slope)).astype(BF16))
    dz1s = [(mm_nt(dz2, w2) * slope).astype(BF16) for dz2, (_, slope) in zip(dz2s, first)]
    if ready is not None:
        ready()
    g2_ref[...] += mm_tn(stack(a1s), stack(dz2s))
    g1_ref[...] += mm_tn(stack(xs), stack(dz1s))
    if summed is not None:
        summed()
    return [mm_nt(dz1, w1) for dz1 in dz1s]


def scores(ws_ref):
    ws = ws_ref[...].astype(F32)
    return jnp.transpose(jnp.broadcast_to(ws, (LANES, WIDTH))).astype(BF16), ws * 0.5


def positive_kernel(recv_ref, emb_ref, w1_hbm, w2_hbm, ws_ref, ec_ref,
                    ret_ref, gdst_hbm, row_ref, g1_hbm, g2_hbm, gs_ref, loss_ref,
                    w1_ref, w2_ref, gdst_ref, g1_ref, g2_ref, sems, out_sems):
    ins = [pltpu.make_async_copy(a, b, sems.at[i]) for i, (a, b) in enumerate([(w1_hbm, w1_ref), (w2_hbm, w2_ref)])]
    for copy in ins:
        copy.start()
    _, total = counts(ec_ref)
    wsb, wsr = scores(ws_ref)
    g1_ref[...] = jnp.zeros_like(g1_ref)
    g2_ref[...] = jnp.zeros_like(g2_ref)
    gs_ref[...] = jnp.zeros_like(gs_ref)
    loss_ref[...] = jnp.zeros_like(loss_ref)
    spread = iota((LANES, 2 * LANES), 0)
    right = iota((LANES, 2 * LANES), 1) >= LANES
    table = jnp.where(
        right,
        jnp.where(spread == 2, 1.0, 0.0),
        jnp.where(spread == 0, 64.0, jnp.where(spread == 1, 1.0, 0.0)),
    ).astype(BF16)
    lane = iota((8, LANES), 1)
    sub = iota((8, LANES), 0)
    flag = jnp.where(jnp.logical_and(sub == 0, lane == 2), 1.0, 0.0).astype(BF16)
    taken = mm_nt(flag, recv_ref[:, WIDTH:WIDE])[0:1, :]
    taken = jnp.concatenate([taken[:, LANES * j:LANES * (j + 1)] for j in range(8)], axis=0)
    before = one(iota((LANES, LANES), 0) < iota((LANES, LANES), 1))
    place = mm(taken.astype(BF16), before)
    held = jnp.broadcast_to(jnp.sum(taken, axis=1, keepdims=True), (8, LANES))
    offset = jnp.zeros((8, LANES), F32)
    for j in range(7):
        offset = offset + jnp.where(sub > j, held[j:j + 1, :], 0.0)
    place = jnp.where(taken > 0.5, place + offset, -1.0).astype(jnp.int32)
    place = jnp.concatenate([place[j:j + 1, :] for j in range(8)], axis=1)
    place_col = column(place)
    half = SLOTS // 2
    rounds = jnp.where(jnp.sum(taken) > half, 2, 1)
    row_ref[...] = jnp.full(row_ref.shape, -1.0, F32)
    ret_ref[...] = jnp.zeros_like(ret_ref)

    def step(h, carry):
        rows = pl.ds(pl.multiple_of(h * half, half), half)
        chosen = one(iota((half, SLOTS), 0) + h * half == place)
        got = mm(chosen, recv_ref[...])
        src = got[:, 0:WIDTH]
        told = mm(got[:, WIDTH:].astype(BF16), table)
        live = told[:, LANES:]
        row = jnp.where(live > 0.5, told[:, :LANES], -1.0)
        row_ref[:, rows] = jnp.transpose(row)[0:8, :]
        dst = mm(onehot_rows(row.astype(jnp.int32), ROWS), emb_ref[...])

        def head(score, a2):
            loss_ref[...] += jnp.sum(live * softplus(-score), axis=0, keepdims=True) / total
            ds = -live * jax.nn.sigmoid(-score) / total
            gs_ref[...] += jnp.sum(wide(ds) * a2, axis=0, keepdims=True)
            return ds

        outs = [
            pltpu.make_async_copy(g1_ref, g1_hbm, out_sems.at[0]),
            pltpu.make_async_copy(g2_ref, g2_hbm, out_sems.at[1]),
            pltpu.make_async_copy(gdst_ref.at[rows, :], gdst_hbm.at[rows, :], out_sems.at[2]),
        ]

        def summed():
            for copy in outs[:2]:
                copy.start()

        @pl.when(h == 0)
        def _():
            for copy in ins:
                copy.wait()

        w1 = w1_ref[...] * BF16(0.5)
        w2 = w2_ref[...] * BF16(0.5)

        (dx,) = decode_parts([(src * dst).astype(BF16)], [head], w1, w2, wsb, wsr, g1_ref, g2_ref, None, summed)
        dx = dx * 2.0
        gdst_ref[rows, :] = (dx * src).astype(BF16)
        outs[2].start()
        back = mm(onehot_rows(place_col - h * half, half), (dx * dst).astype(BF16))
        ret_ref[...] = (ret_ref[...].astype(F32) + back).astype(BF16)
        for copy in outs:
            copy.wait()
        return carry

    lax.fori_loop(0, rounds, step, 0)


def positive(recv, emb, w1, w2, ws, ec):
    return pl.pallas_call(
        positive_kernel,
        in_specs=[VMEM, VMEM, HBM, HBM, VMEM, VMEM],
        out_specs=[VMEM, HBM, VMEM, HBM, HBM, VMEM, VMEM],
        out_shape=[
            pltpu.VMEM((SLOTS, WIDTH), BF16),
            pltpu.HBM((SLOTS, WIDTH), BF16),
            jax.ShapeDtypeStruct((8, SLOTS), F32),
            pltpu.HBM((WIDTH, WIDTH), F32),
            pltpu.HBM((WIDTH, WIDTH), F32),
            jax.ShapeDtypeStruct((1, WIDTH), F32),
            jax.ShapeDtypeStruct((1, LANES), F32),
        ],
        scratch_shapes=[
            pltpu.VMEM((WIDTH, WIDTH), BF16),
            pltpu.VMEM((WIDTH, WIDTH), BF16),
            pltpu.VMEM((SLOTS, WIDTH), BF16),
            pltpu.VMEM((WIDTH, WIDTH), F32),
            pltpu.VMEM((WIDTH, WIDTH), F32),
            pltpu.SemaphoreType.DMA((2,)),
            pltpu.SemaphoreType.DMA((3,)),
        ],
        compiler_params=pltpu.CompilerParams(vmem_limit_bytes=36 * MIB),
        cost_estimate=pl.CostEstimate(flops=6_000_000_000, bytes_accessed=12 * MIB, transcendentals=0),
        name="positive",
    )(recv, emb, *in_hbm(w1, w2), ws, ec)


def negative_kernel(semb_ref, neg_ref, w1_ref, w2_ref, ws_ref, ec_ref, g1_in, g2_in, gs_in, loss_in,
                    keep_hbm, send_ref, gsrc_hbm, extra_ref, gsrc_ref, g1_ref, g2_ref, gs_ref, loss_ref, gneg_ref,
                    sems):
    ins = [pltpu.make_async_copy(a, b, sems.at[i]) for i, (a, b) in enumerate([(g1_in, g1_ref), (g2_in, g2_ref)])]
    for copy in ins:
        copy.start()
    mine, total = counts(ec_ref)
    wsb, wsr = scores(ws_ref)
    gs_ref[...] = gs_in[...]
    loss_ref[...] = loss_in[...]
    gsrc_ref[...] = jnp.zeros_like(gsrc_ref)
    scale = 1.0 / (NEG * total)
    live = jnp.where(iota((EDGES, LANES), 0).astype(F32) < mine, scale, 0.0)

    def head(score, a2):
        loss_ref[...] += jnp.sum(live * softplus(score), axis=0, keepdims=True)
        ds = live * jax.nn.sigmoid(score)
        gs_ref[...] += jnp.sum(wide(ds) * a2, axis=0, keepdims=True)
        return ds

    w1 = w1_ref[...] * BF16(0.5)
    w2 = w2_ref[...] * BF16(0.5)

    def step(i, carry):
        src = semb_ref[...].astype(F32)
        ks = [4 * i + j for j in range(4)]
        negs = [neg_ref[pl.ds(k, 1), :] for k in ks]
        xs = [(src * n).astype(BF16) for n in negs]

        def ready():
            @pl.when(i == 0)
            def _():
                for copy in ins:
                    copy.wait()

        dxs = decode_parts(xs, [head] * 4, w1, w2, wsb, wsr, g1_ref, g2_ref, ready)
        gsrc = gsrc_ref[...]
        for k, n, dx in zip(ks, negs, dxs):
            gsrc = gsrc + dx * n
            gneg_ref[pl.ds(k, 1), :] = jnp.sum(dx * src, axis=0, keepdims=True)
        gsrc_ref[...] = gsrc
        return carry

    lax.fori_loop(0, NEG // 4, step, 0)
    out = pltpu.make_async_copy(gsrc_ref, gsrc_hbm, sems.at[2])
    out.start()
    loss = jnp.concatenate([loss_ref[...], jnp.zeros((1, WIDTH - LANES), F32)], axis=1)
    extra = jnp.concatenate([gneg_ref[...] * 2.0, gs_ref[...], loss, jnp.zeros((6, WIDTH), F32)], axis=0)
    extra_ref[...] = extra
    send_ref[WIDTH:, :] = extra
    core = lax.axis_index("c")
    for at, (kept, sent) in enumerate([(g1_ref, g2_ref), (g2_ref, g1_ref)]):
        @pl.when(core == at)
        def _():
            copy = pltpu.make_async_copy(kept, keep_hbm, sems.at[3])
            copy.start()
            send_ref[0:WIDTH, :] = sent[...]
            copy.wait()

    out.wait()


def negative(semb, negs, w1, w2, ws, ec, g1, g2, gs, loss):
    return pl.pallas_call(
        negative_kernel,
        in_specs=[VMEM] * 6 + [HBM] * 2 + [VMEM] * 2,
        out_specs=[HBM, VMEM, HBM, VMEM],
        out_shape=[
            pltpu.HBM((WIDTH, WIDTH), F32),
            jax.ShapeDtypeStruct((TALL, WIDTH), F32),
            pltpu.HBM((EDGES, WIDTH), F32),
            jax.ShapeDtypeStruct((TALL - WIDTH, WIDTH), F32),
        ],
        scratch_shapes=[pltpu.VMEM((WIDTH, WIDTH), F32)] * 3 + [
            pltpu.VMEM((1, WIDTH), F32),
            pltpu.VMEM((1, LANES), F32),
            pltpu.VMEM((NEG, WIDTH), F32),
            pltpu.SemaphoreType.DMA((4,)),
        ],
        compiler_params=pltpu.CompilerParams(vmem_limit_bytes=40 * MIB),
        cost_estimate=pl.CostEstimate(flops=20_000_000_000, bytes_accessed=8 * MIB, transcendentals=0),
        name="negative",
    )(semb, negs, w1, w2, ws, ec, *in_hbm(g1, g2), gs, loss)


def join_kernel(keep_hbm, got_ref, mine_ref, out_ref, keep_ref, sems):
    count = WIDTH // 4
    copies = []
    for q in range(4):
        rows = pl.ds(q * count, count)
        copies.append(pltpu.make_async_copy(keep_hbm.at[rows, :], keep_ref.at[rows, :], sems.at[q]))
        copies[q].start()
    extra = mine_ref[...] + got_ref[WIDTH:, :]
    tiles = []
    for k in range(NEG + 2):
        block = jnp.concatenate([extra[k:k + 1, LANES * j:LANES * (j + 1)] for j in range(4)], axis=0)
        high = block.astype(BF16).astype(F32)
        tiles += [high, block - high]
    tiles.append(jnp.zeros((WIDTH - 8 * (NEG + 2), LANES), F32))
    out_ref[:, WIDTH:] = stack(tiles).astype(BF16)
    for q in range(4):
        rows = pl.ds(q * count, count)
        copies[q].wait()
        out_ref[rows, 0:WIDTH] = (keep_ref[rows, :] + got_ref[rows, :]).astype(BF16)


def join(keep, got, mine):
    return pl.pallas_call(
        join_kernel,
        in_specs=[HBM, VMEM, VMEM],
        out_specs=VMEM,
        out_shape=jax.ShapeDtypeStruct((WIDTH, WIDE), BF16),
        scratch_shapes=[pltpu.VMEM((WIDTH, WIDTH), F32), pltpu.SemaphoreType.DMA((4,))],
        compiler_params=pltpu.CompilerParams(vmem_limit_bytes=16 * MIB),
        name="join",
    )(*in_hbm(keep), got, mine)


def block_of(node):
    local = node - lax.axis_index(AXES) * ROWS
    held = jnp.logical_and(local >= 0, local < ROWS)
    return held, jnp.where(held, local // 8 * 8, 0)


def scatter_kernel(gsrc_ref, back_ref, pos_ref, src_ref, gdst_ref, row_ref, neg_ref,
                   out_ref, near_ref, shi, slo, dst):
    block = out_ref.shape[0]

    @pl.when(pl.program_id(0) == 0)
    def _():
        placed = onehot_rows(column(pos_ref[...]), SLOTS)
        used = column(row_ref[0:1, :]) >= 0
        dst[...] = jnp.where(wide(used.astype(F32)) > 0.5, gdst_ref[...].astype(F32), 0.0).astype(BF16)
        shi[...], slo[...] = split(gsrc_ref[...] * 2.0 + mm(placed, back_ref[...]))
        near_ref[...] = jnp.zeros_like(near_ref)

    base = pl.program_id(0) * block
    mine = one(iota((block, EDGES), 0) + base == src_ref[...])
    theirs = one(iota((block, SLOTS), 0) + base == row_ref[0:1, :].astype(jnp.int32))
    out_ref[...] = (mm(mine, shi[...]) + mm(mine, slo[...])) + mm(theirs, dst[...])
    for k in range(NEG):
        held, at = block_of(neg_ref[k])

        @pl.when(jnp.logical_and(held, jnp.logical_and(at >= base, at < base + block)))
        def _():
            near_ref[k] = out_ref[pl.ds(pl.multiple_of(jnp.clip(at - base, 0, block - 8), 8), 8), :]


def scatter(gsrc, back, pos, src_row, gdst, rows, neg_ids):
    block = 512
    whole = lambda shape: pl.BlockSpec(shape, lambda i: (0, 0))
    return pl.pallas_call(
        scatter_kernel,
        grid=(ROWS // block,),
        in_specs=[
            whole((EDGES, WIDTH)), whole((SLOTS, WIDTH)), whole((1, EDGES)),
            whole((1, EDGES)), whole((SLOTS, WIDTH)), whole((8, SLOTS)), SMEM,
        ],
        out_specs=[pl.BlockSpec((block, WIDTH), lambda i: (i, 0)), pl.BlockSpec((NEG, 8, WIDTH), lambda i: (0, 0, 0))],
        out_shape=[jax.ShapeDtypeStruct((ROWS, WIDTH), F32), jax.ShapeDtypeStruct((NEG, 8, WIDTH), F32)],
        scratch_shapes=[
            pltpu.VMEM((EDGES, WIDTH), BF16), pltpu.VMEM((EDGES, WIDTH), BF16),
            pltpu.VMEM((SLOTS, WIDTH), BF16),
        ],
        compiler_params=pltpu.CompilerParams(vmem_limit_bytes=24 * MIB),
        cost_estimate=pl.CostEstimate(flops=7_000_000_000, bytes_accessed=10 * MIB, transcendentals=0),
        name="scatter",
    )(gsrc, back, pos, src_row, gdst, rows, neg_ids)


def total_kernel(parts_ref, out_ref):
    def step(i, acc):
        rows = pl.ds(pl.multiple_of(i * 64, 64), 64)
        part = parts_ref[rows, :].astype(F32)
        for j in range(8):
            acc = acc + part[8 * j:8 * j + 8, :]
        return acc

    acc = lax.fori_loop(0, GROUP // 8, step, jnp.zeros((CAP, WIDE), F32))
    extra = acc[:, WIDTH:]
    extra = extra[0:4, :] + extra[4:8, :]
    high = extra.astype(BF16).astype(F32)
    line = jnp.concatenate([acc[:, :WIDTH], jnp.concatenate([high, extra - high], axis=0)], axis=1)
    both = jnp.concatenate([line, line], axis=0).astype(BF16)

    def store(i, carry):
        out_ref[pl.ds(pl.multiple_of(i * 16, 16), 16), :] = both
        return carry

    lax.fori_loop(0, GROUP // 2, store, 0)


def total_up(parts):
    return pl.pallas_call(
        total_kernel,
        in_specs=[VMEM],
        out_specs=VMEM,
        out_shape=jax.ShapeDtypeStruct((WIDTH, WIDE), BF16),
        compiler_params=pltpu.CompilerParams(vmem_limit_bytes=16 * MIB),
        name="total_up",
    )(parts)


def sent_out(sums_ref, f_ref, out_hbm, sems):
    copies = []
    for h in range(4):
        rows = pl.ds(h * 128, 128)
        f_ref[rows, :] = sums_ref[rows, 0:WIDTH].astype(F32)
        copies.append(pltpu.make_async_copy(f_ref.at[rows, :], out_hbm.at[rows, :], sems.at[h]))
        copies[h].start()
    return copies


def own_kernel(sums_ref, neg_ref, near_ref, grads_in, g1_hbm, g2_hbm, gs_ref, loss_ref, grads_ref, half_ref, blocks, sems, out_sems):
    mine, bases = zip(*[block_of(neg_ref[k]) for k in range(NEG)])
    me = lax.axis_index(AXES)

    def put(k):
        rows = pl.ds(pl.multiple_of(bases[k], 8), 8)
        return pltpu.make_async_copy(blocks.at[k], grads_ref.at[rows, :], sems.at[k])

    extra = sums_ref[0:8 * (NEG + 2), WIDTH:].astype(F32)

    def line(k):
        block = extra[8 * k:8 * k + 4, :] + extra[8 * k + 4:8 * k + 8, :]
        return jnp.concatenate([block[j:j + 1, :] for j in range(4)], axis=1)

    gs_ref[...] = line(NEG)
    loss_ref[...] = line(NEG + 1)[:, 0:LANES]
    sub = iota((8, WIDTH), 0)
    for k in range(NEG):
        block = near_ref[k]
        for j in range(NEG):
            local = neg_ref[j] - me * ROWS
            hit = jnp.logical_and(mine[j], bases[j] == bases[k])
            at = jnp.where(hit, local - bases[k], -1)
            block = block + jnp.where(sub == at, line(j), 0.0)
        blocks[k] = block

        @pl.when(mine[k])
        def _():
            put(k).start()

    core = lax.axis_index("c")
    for at, g_hbm in enumerate([g1_hbm, g2_hbm]):
        @pl.when(core == at)
        def _():
            sent_out(sums_ref, half_ref, g_hbm, out_sems.at[at])

    for k in range(NEG):
        @pl.when(mine[k])
        def _():
            put(k).wait()

    for at, g_hbm in enumerate([g1_hbm, g2_hbm]):
        @pl.when(core == at)
        def _():
            for h in range(4):
                rows = pl.ds(h * 128, 128)
                pltpu.make_async_copy(half_ref.at[rows, :], g_hbm.at[rows, :], out_sems.at[at, h]).wait()


def finish_own(sums, neg_ids, near, grads):
    return pl.pallas_call(
        own_kernel,
        in_specs=[VMEM, SMEM, VMEM, pl.BlockSpec(memory_space=pl.ANY)],
        out_specs=[HBM, HBM, VMEM, VMEM, pl.BlockSpec(memory_space=pl.ANY)],
        out_shape=[
            pltpu.HBM((WIDTH, WIDTH), F32),
            pltpu.HBM((WIDTH, WIDTH), F32),
            jax.ShapeDtypeStruct((1, WIDTH), F32),
            jax.ShapeDtypeStruct((1, LANES), F32),
            jax.ShapeDtypeStruct((ROWS, WIDTH), F32),
        ],
        input_output_aliases={3: 4},
        scratch_shapes=[
            pltpu.VMEM((WIDTH, WIDTH), F32),
            pltpu.VMEM((NEG, 8, WIDTH), F32),
            pltpu.SemaphoreType.DMA((NEG,)),
            pltpu.SemaphoreType.DMA((2, 4)),
        ],
        compiler_params=pltpu.CompilerParams(vmem_limit_bytes=16 * MIB),
        cost_estimate=pl.CostEstimate(flops=1_000_000, bytes_accessed=2 * MIB, transcendentals=0),
        name="finish_own",
    )(sums, neg_ids, near, grads)


def other_kernel(other_ref, g1_in, g2_in, g1_hbm, g2_hbm, rest_ref, sems):
    core = lax.axis_index("c")
    for at, g_hbm in enumerate([g2_hbm, g1_hbm]):
        @pl.when(core == at)
        def _():
            for copy in sent_out(other_ref, rest_ref, g_hbm, sems.at[at]):
                copy.wait()


def finish_other(other, g1, g2):
    return pl.pallas_call(
        other_kernel,
        in_specs=[VMEM, HBM, HBM],
        out_specs=[HBM, HBM],
        out_shape=[pltpu.HBM((WIDTH, WIDTH), F32)] * 2,
        input_output_aliases={1: 0, 2: 1},
        scratch_shapes=[pltpu.VMEM((WIDTH, WIDTH), F32), pltpu.SemaphoreType.DMA((2, 4))],
        compiler_params=pltpu.CompilerParams(vmem_limit_bytes=16 * MIB),
        name="finish_other",
    )(other, *in_hbm(g1, g2))


def exchange(rows, axes):
    parts = rows.reshape(-1, CAP, rows.shape[1])
    out = lax.all_to_all(parts, axes, split_axis=0, concat_axis=0, tiled=True)
    return out.reshape(rows.shape)


def swap(rows):
    return lax.ppermute(rows, "c", [(0, 1), (1, 0)])


def complete(rows):
    rows = rows + swap(rows)
    got = [lax.ppermute(rows, "x", [(i, (i + by) % 4) for i in range(4)]) for by in (1, 2, 3)]
    return (rows + got[0]) + (got[1] + got[2])


def body(embeddings, w_first, w_second, w_score, src_row, dst_owner, dst_row, edge_count, neg_ids):
    ec = edge_count.reshape(1, DEVICES)
    ws = w_score.reshape(1, WIDTH)
    src_row = src_row.reshape(1, EDGES)
    push, semb, pos = prepare(
        embeddings, src_row, dst_owner.reshape(1, EDGES), dst_row.reshape(1, EDGES), ec, neg_ids
    )
    recv = exchange(push, AXES)
    negs = complete(pick(recv))
    ret, gdst, rows, g1, g2, gs, loss = positive(recv, embeddings, w_first, w_second, ws, ec)
    back = exchange(ret, AXES)
    keep, send, gsrc, extra = negative(semb, negs, w_first, w_second, ws, ec, g1, g2, gs, loss)
    send, back = lax.optimization_barrier((send, back))
    payload = join(keep, swap(send), extra)
    parts = exchange(payload, CHIPS)
    grads, near = scatter(gsrc, back, pos, src_row, gdst, rows, neg_ids)
    parts, grads = lax.optimization_barrier((parts, grads))
    sums = exchange(total_up(parts), CHIPS)
    other = swap(sums)
    g1, g2, gs, loss, grads = finish_own(sums, neg_ids, near, grads)
    g1, g2 = finish_other(other, g1, g2)
    return grads, g1, g2, gs.reshape(WIDTH), loss[0, 0]


def solution(mesh):
    mesh = Mesh(mesh.devices.reshape(4, 4, 2, 4), AXES)
    in_specs = (
        P(AXES, None), P(), P(), P(), P(AXES), P(AXES, None), P(AXES), P(), P(),
    )
    out_specs = (P(AXES, None), P(), P(), P(), P())
    return jax.shard_map(body, mesh=mesh, in_specs=in_specs, out_specs=out_specs, check_vma=False)
```

time: 359 us -> 133 us (0.37)
  blocking collectives: 135 us -> 52 us
  other arithmetic: 59.6 us -> 0.01 us
  waiting for transfers between devices: 63.8 us -> 7.46 us
  Pallas kernels: 0 us -> 46.6 us
  matrix products: 39.2 us -> 0 us
  local copies, waits for them, and re-layouts: 22.4 us -> 2.36 us
  between operations: 16.4 us -> 1.04 us
    psum x2 -> x0, blocking collectives: 135 us -> none  [the longest x1 68 us: body(): lax.psum((grad_neg, grad_first, grad_second, grad_score, loss), ('node',...]
    all_to_all x0 -> x2, blocking collectives: none -> 52 us  [exchange(): out = lax.all_to_all(parts, axes, split_axis=0, concat_axis=0, tiled=True)]
    psum x1 -> x0, waiting for transfers between devices: 49.6 us -> none  [body(): lax.psum((grad_neg, grad_first, grad_second, grad_score, loss), ('node',...]
    pallas_call x0 -> x9, Pallas kernels: none -> 46.6 us  [the longest x1 20.5 us: negative(): pl.pallas_call(negative_kernel, in_specs=[VMEM] * 6 + [HBM] * 2 + [VMEM]...]
    dot_general x8 -> x0, matrix products: 39.2 us -> none  [the longest x1 8.06 us: decode(): z_one = jnp.dot(stacked, w_first, preferred_element_type=jnp.float32)]
    scatter-add x3 -> x0, other arithmetic: 23.4 us -> none  [the longest x1 11.7 us: body(): grads.at[wanted.reshape(-1)].add(arrived.reshape(devices * capacity, width))]
    convert_element_type x5 -> x0, other arithmetic: 12.1 us -> none  [the longest x1 7.33 us: decode(): (slope[:, None] * w_score.astype(jnp.float32)[None, :] * silu_slope(z_two...]
    dot_general x2 -> x0, other arithmetic: 10.7 us -> none  [the longest x1 6.36 us: decode(): grad_src = dx_pos * dst_f + jnp.einsum('ekd,kd->ed', dx_neg, neg_f)]
  transfers between devices with their start and end apart: 4 -> 8, of which waited for: 2 -> 3; matrix products, arithmetic and copies ran while one was open for 16% -> 0% of each run, Pallas kernels for 0% -> 29%
where the time goes in v1:
time: 133 us; the launch traced here: 132 us
  blocking collectives  52 us (39%)
  Pallas kernels  46.6 us (35%)
  starting transfers between devices  22.7 us (17%)
  waiting for transfers between devices  7.46 us (6%)
  local copies, waits for them, and re-layouts  2.36 us (2%)
    all_to_all x2, blocking collectives, exchange(): out = lax.all_to_all(parts, axes, split_axis=0, concat_axis=0, tiled=True)  52 us
    pallas_call x1, Pallas kernels, negative(): pl.pallas_call(negative_kernel, in_specs=[VMEM] * 6 + [HBM] * 2 + [VMEM]...  20.5 us
    all_to_all x2, starting transfers between devices, exchange(): out = lax.all_to_all(parts, axes, split_axis=0, concat_axis=0, tiled=True)  15.7 us
    pallas_call x1, Pallas kernels, scatter(): pl.pallas_call(scatter_kernel, grid=(ROWS // block,), in_specs=[whole((ED...  8.06 us
    pallas_call x1, Pallas kernels, positive(): pl.pallas_call(positive_kernel, in_specs=[VMEM, VMEM, HBM, HBM, VMEM, VME...  7.78 us
    all_to_all x2, waiting for transfers between devices, exchange(): out = lax.all_to_all(parts, axes, split_axis=0, concat_axis=0, tiled=True)  4.34 us
    ppermute x3, starting transfers between devices, swap(): return lax.ppermute(rows, 'c', [(0, 1), (1, 0)])  4.17 us
    pallas_call x1, Pallas kernels, prepare(): pl.pallas_call(prepare_kernel, in_specs=[HBM] * 6, out_specs=[VMEM, HBM,...  4.12 us
  transfers between devices with their start and end apart: 8, of which 3 were waited for; matrix products, arithmetic and copies ran while one was open for 0% of the time, Pallas kernels for 29%

profile of v1, /device:TPU:1, one launch (start us, length us, event | category | flops | bytes accessed | tf_op | source)
XLA Modules:
  0.0 132.1 jit_solution(16010325714972061039)
XLA Ops:
  0.6 4.1 %prepare.1 = (bf16[1024,640]{1,0:T(8,128)(2,1)S(1)}, bf16[512,512]{1,0:T(8,128)(2,1)}, s32[1,512]{1,0:T(1,128)S(1)}) custom-call(bf16[2048,512]{1,0:T(8,128)(2,1)} %emb_ref.1, s32[1,512]{1,0:T(1,128)} %bitcast.23, s32[1,512]{1,0:T(1,128)} %bitcast.28, s32[1,512]{1,0:T(1,128)} %bitcast.29, s32[1,128]{1,0:T(1,128)} %bitcast.25, s32[8]{0:T(128)} %neg_ref.3), custom_call_target="tpu_custom_call" | custom-call | tf_op jit(solution)/shard_map/prepare/pallas_call | solution.py:141
  4.8 0.0 copy-start
  4.8 33.7 %all_to_all.20 = bf16[128,8,640]{2,1,0:T(8,128)(2,1)S(1)} all-to-all(bf16[128,8,640]{2,1,0:T(8,128)(2,1)S(1)} %bitcast.21), channel_id=1, replica_groups=mesh['z'=4,'y'=4,'c'=2,'x'=4] {'z','y','c','x'}, dimensions={0} | all-to-all | bytes 2621440 | tf_op jit(solution)/shard_map/all_to_all | solution.py:641
  38.5 0.0 copy-start.9
  38.5 0.0 copy-start.3
  38.5 0.2 pick.1
  38.7 0.4 collective-permute-start
  39.1 0.1 copy-done.9
  39.2 0.8 collective-permute-done
  39.9 0.3 collective-permute-start.1
  40.2 2.0 %collective-permute-start.2 = (f32[8,512]{1,0:T(8,128)S(1)}, f32[8,512]{1,0:T(8,128)S(1)}, u32[]{:S(2)}, u32[]{:S(2)}) collective-permute-start(f32[8,512]{1,0:T(8,128)S(1)} %add.12), channel_id=1, source_target_pairs={{0,2},{1,3},{2,0},{3,1},{4,6},{5,7},{6,4},{7,5},{8,10},{9,11},{10,... | collective-permute-start | bytes 49160 | tf_op jit(solution)/shard_map/ppermute | solution.py:651
  42.3 0.5 collective-permute-start.3
  42.7 0.0 copy-done
  42.7 0.0 copy-done.3
  42.7 7.8 %positive.1 = (bf16[1024,512]{1,0:T(8,128)(2,1)}, bf16[1024,512]{1,0:T(8,128)(2,1)}, f32[8,1024]{1,0:T(8,128)S(1)}, f32[512,512]{1,0:T(8,128)}, f32[512,512]{1,0...) custom-call(bf16[1024,640]{1,0:T(8,128)(2,1)S(1)} %bitcast.16, bf16[2048,512]{1,0:T(8,128)(2,1)S(1)} %copy-done, ...), custom_call_target="tpu_custom_call" | custom-call | flops 6000000000 | bytes 12582912 | tf_op jit(solution)/shard_map/positive/pallas_call | solution.py:302
  50.5 0.0 copy-start.4
  50.5 0.0 copy-start.5
  50.5 5.7 %all-to-all-start.1 = ((bf16[128,8,512]{2,1,0:T(8,128)(2,1)}), bf16[128,8,512]{2,1,0:T(8,128)(2,1)S(1)}, u32[]{:S(2)}, u32[]{:S(2)}) async-start(bf16[128,8,512]{2,1,0:T(8,128)(2,1)} %bitcast.6), calls=%async_computation.1 | async-start | bytes 2097152 | tf_op jit(solution)/shard_map/all_to_all | solution.py:641
  56.2 0.0 collective-permute-done.1
  56.2 0.0 collective-permute-done.2
  56.2 0.0 collective-permute-done.3
  56.3 0.0 copy-done.4
  56.3 0.0 copy-done.5
  56.3 0.0 copy-start.6
  56.3 1.0 copy-done.6
  57.3 20.5 %negative.1 = (f32[512,512]{1,0:T(8,128)}, f32[528,512]{1,0:T(8,128)S(1)}, f32[512,512]{1,0:T(8,128)}, f32[16,512]{1,0:T(8,128)S(1)}) custom-call(bf16[512,512]{1,0:T(8,128)(2,1)S(1)} %copy-done.6, f32[8,512]{1,0:T(8,128)S(1)} %add_add_fusion.neg_ref, bf16[512,512]{1,0:T(8,128)(2,1)S(1)} %copy-done.4, bf16[512,512]{1,0:T(8,128)(2,1)S(1)} %copy-done.5, ...), custom_call_target="tpu_custom_call" | custom-call | flops 20000000000 | bytes 8388608 | tf_op jit(solution)/shard_map/negative/pallas_call | solution.py:393
  77.8 0.0 all-to-all-done.1
  77.8 1.3 collective-permute-start.4
  79.2 2.3 %collective-permute-done.4.got_ref = f32[528,512]{1,0:T(8,128)S(1)} collective-permute-done((f32[528,512]{1,0:T(8,128)S(1)}, f32[528,512]{1,0:T(8,128)S(1)}, u32[]{:S(2)}, u32[]{:S(2)}) %collective-permute-start.4) | collective-permute-done | bytes 1081376 | tf_op jit(solution)/shard_map/ppermute | solution.py:646
  81.5 2.1 %join.1 = bf16[512,640]{1,0:T(8,128)(2,1)} custom-call(f32[512,512]{1,0:T(8,128)} %get-tuple-element.38.keep_hbm, f32[528,512]{1,0:T(8,128)S(1)} %collective-permute-done.4.got_ref, f32[16,512]{1,0:T(8,128)S(1)} %get-tuple-element.42.mine_ref), custom_call_target="tpu_custom_call" | custom-call | tf_op jit(solution)/shard_map/join/pallas_call | solution.py:437
  83.6 0.0 copy-start.1
  83.6 0.0 copy-start.2
  83.6 0.0 copy-start.7
  83.6 10.0 %all-to-all-start.2 = ((bf16[64,8,640]{2,1,0:T(8,128)(2,1)}), bf16[64,8,640]{2,1,0:T(8,128)(2,1)S(1)}, u32[]{:S(2)}, u32[]{:S(2)}) async-start(bf16[64,8,640]{2,1,0:T(8,128)(2,1)} %bitcast.8), calls=%async_computation.2 | async-start | bytes 1310720 | tf_op jit(solution)/shard_map/all_to_all | solution.py:641
  93.7 0.0 copy-done.1
  93.7 0.0 copy-done.2
  93.7 0.0 copy-done.7
  93.7 0.0 copy-start.8
  93.7 1.2 copy-done.8
  94.9 8.1 %scatter.1 = (f32[2048,512]{1,0:T(8,128)}, f32[8,8,512]{2,1,0:T(8,128)S(1)}) custom-call(f32[512,512]{1,0:T(8,128)S(1)} %copy-done.8, bf16[1024,512]{1,0:T(8,128)(2,1)S(1)} %bitcast.22, s32[1,512]{1,0:T(1,128)S(1)} %get-tuple-element.45.pos_ref, s32[1,512]{1,0:T(1,128)S(1)} %bitcast.24, bf16[1024,512]{1,0:T(8,128)(2,1)S(1)} %copy-done.7, ...), custom_call_target="tpu_custom_call" | custom-call | flops 7000000000 | bytes 10485760 | tf_op jit(solution)/shard_map/scatter/pallas_call | solution.py:481
  103.0 4.3 %all-to-all-done.2 = bf16[64,8,640]{2,1,0:T(8,128)(2,1)S(1)} async-done(((bf16[64,8,640]{2,1,0:T(8,128)(2,1)}), bf16[64,8,640]{2,1,0:T(8,128)(2,1)S(1)}, u32[]{:S(2)}, u32[]{:S(2)}) %all-to-all-start.2) | async-done | bytes 655392 | tf_op jit(solution)/shard_map/all_to_all | solution.py:641
  107.3 0.3 total_up.1
  107.6 18.3 %all_to_all.21 = bf16[64,8,640]{2,1,0:T(8,128)(2,1)S(1)} all-to-all(bf16[64,8,640]{2,1,0:T(8,128)(2,1)S(1)} %bitcast.20), channel_id=1, replica_groups=mesh['z'=4,'y'=4,'c'=2,'x'=4] {'z','y','x'}, dimensions={0} | all-to-all | bytes 1310720 | tf_op jit(solution)/shard_map/all_to_all | solution.py:641
  126.0 2.5 %collective-permute-start.5 = (bf16[512,640]{1,0:T(8,128)(2,1)S(1)}, bf16[512,640]{1,0:T(8,128)(2,1)S(1)}, u32[]{:S(2)}, u32[]{:S(2)}) collective-permute-start(bf16[512,640]{1,0:T(8,128)(2,1)S(1)} %bitcast.17), channel_id=1, source_target_pairs={{0,4},{4,0},{1,5},{5,1},{2,6},{6,2},{3,7},{7,3},{8,12},{12,8},{9,1... | collective-permute-start | bytes 1966088 | tf_op jit(solution)/shard_map/ppermute | solution.py:646
  128.4 2.4 %finish_own.1 = (f32[512,512]{1,0:T(8,128)}, f32[512,512]{1,0:T(8,128)}, f32[1,512]{1,0:T(1,128)}, f32[1,128]{1,0:T(1,128)}, f32[2048,512]{1,0:T(8,128)}) custom-call(bf16[512,640]{1,0:T(8,128)(2,1)S(1)} %bitcast.18, s32[8]{0:T(128)S(1)} %copy-done.2, f32[8,8,512]{2,1,0:T(8,128)S(1)} %get-tuple-element.50.near_ref, ...), custom_call_target="tpu_custom_call", output_to_operand_aliasing={{4}: (3, {})} | custom-call | flops 1000000 | bytes 2097152 | tf_op jit(solution)/shard_map/finish_own/pallas_call | solution.py:593
  130.8 0.0 collective-permute-done.5.other_ref
  130.9 1.1 finish_other.1
  (3 shorter events, 0.0 us)
Async XLA Ops:
  4.8 38.0 %copy-start = (bf16[2048,512]{1,0:T(8,128)(2,1)S(1)}, bf16[2048,512]{1,0:T(8,128)(2,1)}, u32[]{:S(2)}) copy-start(bf16[2048,512]{1,0:T(8,128)(2,1)} %emb_ref.1) | copy-start | bytes 6291460
  38.5 0.7 copy-start.9
  38.5 4.2 %copy-start.3 = (s32[128]{0:T(128)S(1)}, s32[128]{0:T(128)}, u32[]{:S(2)}) copy-start(s32[128]{0:T(128)} %param.16) | copy-start | bytes 1540
  38.7 1.2 collective-permute-start
  39.9 16.3 %collective-permute-start.1 = (f32[8,512]{1,0:T(8,128)S(1)}, f32[8,512]{1,0:T(8,128)S(1)}, u32[]{:S(2)}, u32[]{:S(2)}) collective-permute-start(f32[8,512]{1,0:T(8,128)S(1)} %add.12), channel_id=1, source_target_pairs={{0,1},{1,2},{2,3},{3,0},{4,5},{5,6},{6,7},{7,4},{8,9},{9,10},{10,1... | collective-permute-start | bytes 49160 | tf_op jit(solution)/shard_map/ppermute | solution.py:651
  40.2 16.0 %collective-permute-start.2 = (f32[8,512]{1,0:T(8,128)S(1)}, f32[8,512]{1,0:T(8,128)S(1)}, u32[]{:S(2)}, u32[]{:S(2)}) collective-permute-start(f32[8,512]{1,0:T(8,128)S(1)} %add.12), channel_id=1, source_target_pairs={{0,2},{1,3},{2,0},{3,1},{4,6},{5,7},{6,4},{7,5},{8,10},{9,11},{10,... | collective-permute-start | bytes 49160 | tf_op jit(solution)/shard_map/ppermute | solution.py:651
  42.3 14.0 %collective-permute-start.3 = (f32[8,512]{1,0:T(8,128)S(1)}, f32[8,512]{1,0:T(8,128)S(1)}, u32[]{:S(2)}, u32[]{:S(2)}) collective-permute-start(f32[8,512]{1,0:T(8,128)S(1)} %add.12), channel_id=1, source_target_pairs={{0,3},{1,0},{2,1},{3,2},{4,7},{5,4},{6,5},{7,6},{8,11},{9,8},{10,9... | collective-permute-start | bytes 49160 | tf_op jit(solution)/shard_map/ppermute | solution.py:651
  50.5 5.8 %copy-start.4 = (bf16[512,512]{1,0:T(8,128)(2,1)S(1)}, bf16[512,512]{1,0:T(8,128)(2,1)}, u32[]{:S(2)}) copy-start(bf16[512,512]{1,0:T(8,128)(2,1)} %w1_ref.1) | copy-start | bytes 1572868
  50.5 5.8 %copy-start.5 = (bf16[512,512]{1,0:T(8,128)(2,1)S(1)}, bf16[512,512]{1,0:T(8,128)(2,1)}, u32[]{:S(2)}) copy-start(bf16[512,512]{1,0:T(8,128)(2,1)} %w2_ref.1) | copy-start | bytes 1572868
  50.5 27.3 %all-to-all-start.1 = ((bf16[128,8,512]{2,1,0:T(8,128)(2,1)}), bf16[128,8,512]{2,1,0:T(8,128)(2,1)S(1)}, u32[]{:S(2)}, u32[]{:S(2)}) async-start(bf16[128,8,512]{2,1,0:T(8,128)(2,1)} %bitcast.6), calls=%async_computation.1 | async-start | bytes 2097152 | tf_op jit(solution)/shard_map/all_to_all | solution.py:641
  56.3 1.0 copy-start.6
  77.8 3.6 %collective-permute-start.4 = (f32[528,512]{1,0:T(8,128)S(1)}, f32[528,512]{1,0:T(8,128)S(1)}, u32[]{:S(2)}, u32[]{:S(2)}) collective-permute-start(f32[528,512]{1,0:T(8,128)S(1)} %get-tuple-element.41), channel_id=1, source_target_pairs={{0,4},{4,0},{1,5},{5,1},{2,6},{6,2},{3,7},{7,3},{8,12},{12,8},{9,1... | collective-permute-start | bytes 3244040 | tf_op jit(solution)/shard_map/ppermute | solution.py:646
  83.6 10.1 %copy-start.1 = (s32[512]{0:T(512)S(1)}, s32[512]{0:T(512)}, u32[]{:S(2)}) copy-start(s32[512]{0:T(512)} %param.13) | copy-start | bytes 6148
  83.6 10.1 %copy-start.2 = (s32[8]{0:T(128)S(1)}, s32[8]{0:T(128)}, u32[]{:S(2)}) copy-start(s32[8]{0:T(128)} %neg_ref.3) | copy-start | bytes 100
  83.6 10.1 %copy-start.7 = (bf16[1024,512]{1,0:T(8,128)(2,1)S(1)}, bf16[1024,512]{1,0:T(8,128)(2,1)}, u32[]{:S(2)}) copy-start(bf16[1024,512]{1,0:T(8,128)(2,1)} %get-tuple-element.46.gdst_ref) | copy-start | bytes 3145732
  83.6 23.7 %all-to-all-start.2 = ((bf16[64,8,640]{2,1,0:T(8,128)(2,1)}), bf16[64,8,640]{2,1,0:T(8,128)(2,1)S(1)}, u32[]{:S(2)}, u32[]{:S(2)}) async-start(bf16[64,8,640]{2,1,0:T(8,128)(2,1)} %bitcast.8), calls=%async_computation.2 | async-start | bytes 1310720 | tf_op jit(solution)/shard_map/all_to_all | solution.py:641
  93.7 1.2 copy-start.8
  126.0 4.9 %collective-permute-start.5 = (bf16[512,640]{1,0:T(8,128)(2,1)S(1)}, bf16[512,640]{1,0:T(8,128)(2,1)S(1)}, u32[]{:S(2)}, u32[]{:S(2)}) collective-permute-start(bf16[512,640]{1,0:T(8,128)(2,1)S(1)} %bitcast.17), channel_id=1, source_target_pairs={{0,4},{4,0},{1,5},{5,1},{2,6},{6,2},{3,7},{7,3},{8,12},{12,8},{9,1... | collective-permute-start | bytes 1966088 | tf_op jit(solution)/shard_map/ppermute | solution.py:646

commit v2 on v1

--- a/solution.py
+++ b/solution.py
@@ -109,19 +109,19 @@
     lane = iota((EDGES, LANES), 1)
     meta = jnp.where(lane == 0, row // 64, jnp.where(lane == 1, row % 64, jnp.where(lane == 2, 1, 0)))
     meta = meta.astype(F32).astype(BF16)
-    sub = iota((NEG, LANES), 0)
-    local = jnp.zeros((NEG, LANES), jnp.int32)
+    sub = iota((2 * NEG, LANES), 0)
+    local = jnp.full((2 * NEG, LANES), -1, jnp.int32)
     for k in range(NEG):
         local = jnp.where(sub == k, neg_ref[k] - me * ROWS, local)
-    offered = onehot_rows(local, ROWS)
-    chosen = onehot_rows(column(src_ref[...]), ROWS)
+    chosen = onehot_rows(jnp.concatenate([column(src_ref[...]), local], axis=0), ROWS)
     copies[-1].wait()
     emb = emb_ref[...]
-    semb = mm(chosen, emb).astype(BF16)
+    found = mm(chosen, emb)
+    semb = found[0:EDGES, :].astype(BF16)
     semb_ref[...] = semb
     out = pltpu.make_async_copy(semb_ref, semb_hbm, sems.at[6])
     out.start()
-    offers = mm(offered, emb)
+    offers = found[EDGES:EDGES + NEG, :]
     high = iota((NEG, LANES), 1) >= LANES // 2
     pieces = []
     for q in range(4):
@@ -327,9 +327,12 @@
     )(recv, emb, *in_hbm(w1, w2), ws, ec)
 
 
-def negative_kernel(semb_ref, neg_ref, w1_ref, w2_ref, ws_ref, ec_ref, g1_in, g2_in, gs_in, loss_in,
+def negative_kernel(semb_hbm, neg_ref, w1_ref, w2_ref, ws_ref, ec_ref, g1_in, g2_in, gs_in, loss_in,
                     keep_hbm, send_ref, gsrc_hbm, extra_ref, gsrc_ref, g1_ref, g2_ref, gs_ref, loss_ref, gneg_ref,
-                    sems):
+                    semb_ref, sems):
+    core = lax.axis_index("c")
+    first = pltpu.make_async_copy(semb_hbm, semb_ref, sems.at[4])
+    first.start()
     ins = [pltpu.make_async_copy(a, b, sems.at[i]) for i, (a, b) in enumerate([(g1_in, g1_ref), (g2_in, g2_ref)])]
     for copy in ins:
         copy.start()
@@ -350,6 +353,8 @@
     w1 = w1_ref[...] * BF16(0.5)
     w2 = w2_ref[...] * BF16(0.5)
 
+    first.wait()
+
     def step(i, carry):
         src = semb_ref[...].astype(F32)
         ks = [4 * i + j for j in range(4)]
@@ -362,7 +367,13 @@
                 for copy in ins:
                     copy.wait()
 
-        dxs = decode_parts(xs, [head] * 4, w1, w2, wsb, wsr, g1_ref, g2_ref, ready)
+        def summed():
+            for at, kept in enumerate([g1_ref, g2_ref]):
+                @pl.when(jnp.logical_and(i == NEG // 4 - 1, core == at))
+                def _():
+                    pltpu.make_async_copy(kept, keep_hbm, sems.at[3]).start()
+
+        dxs = decode_parts(xs, [head] * 4, w1, w2, wsb, wsr, g1_ref, g2_ref, ready, summed)
         gsrc = gsrc_ref[...]
         for k, n, dx in zip(ks, negs, dxs):
             gsrc = gsrc + dx * n
@@ -377,14 +388,11 @@
     extra = jnp.concatenate([gneg_ref[...] * 2.0, gs_ref[...], loss, jnp.zeros((6, WIDTH), F32)], axis=0)
     extra_ref[...] = extra
     send_ref[WIDTH:, :] = extra
-    core = lax.axis_index("c")
     for at, (kept, sent) in enumerate([(g1_ref, g2_ref), (g2_ref, g1_ref)]):
         @pl.when(core == at)
         def _():
-            copy = pltpu.make_async_copy(kept, keep_hbm, sems.at[3])
-            copy.start()
             send_ref[0:WIDTH, :] = sent[...]
-            copy.wait()
+            pltpu.make_async_copy(kept, keep_hbm, sems.at[3]).wait()
 
     out.wait()
 
@@ -392,7 +400,7 @@
 def negative(semb, negs, w1, w2, ws, ec, g1, g2, gs, loss):
     return pl.pallas_call(
         negative_kernel,
-        in_specs=[VMEM] * 6 + [HBM] * 2 + [VMEM] * 2,
+        in_specs=[HBM] + [VMEM] * 5 + [HBM] * 2 + [VMEM] * 2,
         out_specs=[HBM, VMEM, HBM, VMEM],
         out_shape=[
             pltpu.HBM((WIDTH, WIDTH), F32),
@@ -404,12 +412,13 @@
             pltpu.VMEM((1, WIDTH), F32),
             pltpu.VMEM((1, LANES), F32),
             pltpu.VMEM((NEG, WIDTH), F32),
-            pltpu.SemaphoreType.DMA((4,)),
+            pltpu.VMEM((EDGES, WIDTH), BF16),
+            pltpu.SemaphoreType.DMA((5,)),
         ],
         compiler_params=pltpu.CompilerParams(vmem_limit_bytes=40 * MIB),
         cost_estimate=pl.CostEstimate(flops=20_000_000_000, bytes_accessed=8 * MIB, transcendentals=0),
         name="negative",
-    )(semb, negs, w1, w2, ws, ec, *in_hbm(g1, g2), gs, loss)
+    )(*in_hbm(semb), negs, w1, w2, ws, ec, *in_hbm(g1, g2), gs, loss)
 
 
 def join_kernel(keep_hbm, got_ref, mine_ref, out_ref, keep_ref, sems):

time: 133 us -> 132 us (level)
  transfers between devices with their start and end apart: 8 -> 8, of which waited for: 3 -> 3; matrix products, arithmetic and copies ran while one was open for 0% -> 0% of each run, Pallas kernels for 29% -> 30%
where the time goes in v2:
time: 132 us; the launch traced here: 131 us
  blocking collectives  52 us (39%)
  Pallas kernels  46.9 us (36%)
  starting transfers between devices  22.6 us (17%)
  waiting for transfers between devices  7.47 us (6%)
  local copies, waits for them, and re-layouts  1.33 us (1%)
    all_to_all x2, blocking collectives, exchange(): out = lax.all_to_all(parts, axes, split_axis=0, concat_axis=0, tiled=True)  52 us
    pallas_call x1, Pallas kernels, negative(): pl.pallas_call(negative_kernel, in_specs=[HBM] + [VMEM] * 5 + [HBM] * 2 +...  21 us
    all_to_all x2, starting transfers between devices, exchange(): out = lax.all_to_all(parts, axes, split_axis=0, concat_axis=0, tiled=True)  15.7 us
    pallas_call x1, Pallas kernels, scatter(): pl.pallas_call(scatter_kernel, grid=(ROWS // block,), in_specs=[whole((ED...  8.06 us
    pallas_call x1, Pallas kernels, positive(): pl.pallas_call(positive_kernel, in_specs=[VMEM, VMEM, HBM, HBM, VMEM, VME...  7.8 us
    all_to_all x2, waiting for transfers between devices, exchange(): out = lax.all_to_all(parts, axes, split_axis=0, concat_axis=0, tiled=True)  4.35 us
    ppermute x3, starting transfers between devices, swap(): return lax.ppermute(rows, 'c', [(0, 1), (1, 0)])  4.19 us
    pallas_call x1, Pallas kernels, prepare(): pl.pallas_call(prepare_kernel, in_specs=[HBM] * 6, out_specs=[VMEM, HBM,...  3.93 us
  transfers between devices with their start and end apart: 8, of which 3 were waited for; matrix products, arithmetic and copies ran while one was open for 0% of the time, Pallas kernels for 30%

profile of v2, /device:TPU:1, one launch (start us, length us, event | category | flops | bytes accessed | tf_op | source)
XLA Modules:
  0.0 131.4 jit_solution(14288038520848248411)
XLA Ops:
  0.6 3.9 %prepare.1 = (bf16[1024,640]{1,0:T(8,128)(2,1)S(1)}, bf16[512,512]{1,0:T(8,128)(2,1)}, s32[1,512]{1,0:T(1,128)S(1)}) custom-call(bf16[2048,512]{1,0:T(8,128)(2,1)} %emb_ref.1, s32[1,512]{1,0:T(1,128)} %bitcast.23, s32[1,512]{1,0:T(1,128)} %bitcast.28, s32[1,512]{1,0:T(1,128)} %bitcast.29, s32[1,128]{1,0:T(1,128)} %bitcast.25, s32[8]{0:T(128)} %neg_ref.3), custom_call_target="tpu_custom_call" | custom-call | tf_op jit(solution)/shard_map/prepare/pallas_call | solution.py:141
  4.6 0.0 copy-start
  4.6 33.7 %all_to_all.20 = bf16[128,8,640]{2,1,0:T(8,128)(2,1)S(1)} all-to-all(bf16[128,8,640]{2,1,0:T(8,128)(2,1)S(1)} %bitcast.21), channel_id=1, replica_groups=mesh['z'=4,'y'=4,'c'=2,'x'=4] {'z','y','c','x'}, dimensions={0} | all-to-all | bytes 2621440 | tf_op jit(solution)/shard_map/all_to_all | solution.py:650
  38.3 0.0 copy-start.8
  38.3 0.0 copy-start.3
  38.3 0.2 pick.1
  38.5 0.4 collective-permute-start
  38.9 0.1 copy-done.8
  39.0 0.8 collective-permute-done
  39.7 0.3 collective-permute-start.1
  40.0 2.0 %collective-permute-start.2 = (f32[8,512]{1,0:T(8,128)S(1)}, f32[8,512]{1,0:T(8,128)S(1)}, u32[]{:S(2)}, u32[]{:S(2)}) collective-permute-start(f32[8,512]{1,0:T(8,128)S(1)} %add.12), channel_id=1, source_target_pairs={{0,2},{1,3},{2,0},{3,1},{4,6},{5,7},{6,4},{7,5},{8,10},{9,11},{10,... | collective-permute-start | bytes 49160 | tf_op jit(solution)/shard_map/ppermute | solution.py:660
  42.1 0.5 collective-permute-start.3
  42.5 0.0 copy-done
  42.5 0.0 copy-done.3
  42.5 7.8 %positive.1 = (bf16[1024,512]{1,0:T(8,128)(2,1)}, bf16[1024,512]{1,0:T(8,128)(2,1)}, f32[8,1024]{1,0:T(8,128)S(1)}, f32[512,512]{1,0:T(8,128)}, f32[512,512]{1,0...) custom-call(bf16[1024,640]{1,0:T(8,128)(2,1)S(1)} %bitcast.16, bf16[2048,512]{1,0:T(8,128)(2,1)S(1)} %copy-done, ...), custom_call_target="tpu_custom_call" | custom-call | flops 6000000000 | bytes 12582912 | tf_op jit(solution)/shard_map/positive/pallas_call | solution.py:302
  50.3 0.0 copy-start.4
  50.3 0.0 copy-start.5
  50.4 5.7 %all-to-all-start.1 = ((bf16[128,8,512]{2,1,0:T(8,128)(2,1)}), bf16[128,8,512]{2,1,0:T(8,128)(2,1)S(1)}, u32[]{:S(2)}, u32[]{:S(2)}) async-start(bf16[128,8,512]{2,1,0:T(8,128)(2,1)} %bitcast.6), calls=%async_computation.1 | async-start | bytes 2097152 | tf_op jit(solution)/shard_map/all_to_all | solution.py:650
  56.0 0.0 collective-permute-done.1
  56.0 0.0 collective-permute-done.2
  56.0 0.0 collective-permute-done.3
  56.1 0.0 copy-done.4
  56.1 0.0 copy-done.5
  56.1 21.0 %negative.1 = (f32[512,512]{1,0:T(8,128)}, f32[528,512]{1,0:T(8,128)S(1)}, f32[512,512]{1,0:T(8,128)}, f32[16,512]{1,0:T(8,128)S(1)}) custom-call(bf16[512,512]{1,0:T(8,128)(2,1)} %get-tuple-element.32.semb_hbm, f32[8,512]{1,0:T(8,128)S(1)} %add_add_fusion.neg_ref, bf16[512,512]{1,0:T(8,128)(2,1)S(1)} %copy-done.4, bf16[512,512]{1,0:T(8,128)(2,1)S(1)} %copy-done.5, ...), custom_call_target="tpu_custom_call" | custom-call | flops 20000000000 | bytes 8388608 | tf_op jit(solution)/shard_map/negative/pallas_call | solution.py:401
  77.1 0.0 all-to-all-done.1
  77.1 1.3 %collective-permute-start.4 = (f32[528,512]{1,0:T(8,128)S(1)}, f32[528,512]{1,0:T(8,128)S(1)}, u32[]{:S(2)}, u32[]{:S(2)}) collective-permute-start(f32[528,512]{1,0:T(8,128)S(1)} %get-tuple-element.41), channel_id=1, source_target_pairs={{0,4},{4,0},{1,5},{5,1},{2,6},{6,2},{3,7},{7,3},{8,12},{12,8},{9,1... | collective-permute-start | bytes 3244040 | tf_op jit(solution)/shard_map/ppermute | solution.py:655
  78.4 2.3 %collective-permute-done.4.got_ref = f32[528,512]{1,0:T(8,128)S(1)} collective-permute-done((f32[528,512]{1,0:T(8,128)S(1)}, f32[528,512]{1,0:T(8,128)S(1)}, u32[]{:S(2)}, u32[]{:S(2)}) %collective-permute-start.4) | collective-permute-done | bytes 1081376 | tf_op jit(solution)/shard_map/ppermute | solution.py:655
  80.8 2.1 %join.1 = bf16[512,640]{1,0:T(8,128)(2,1)} custom-call(f32[512,512]{1,0:T(8,128)} %get-tuple-element.38.keep_hbm, f32[528,512]{1,0:T(8,128)S(1)} %collective-permute-done.4.got_ref, f32[16,512]{1,0:T(8,128)S(1)} %get-tuple-element.42.mine_ref), custom_call_target="tpu_custom_call" | custom-call | tf_op jit(solution)/shard_map/join/pallas_call | solution.py:446
  82.8 0.0 copy-start.1
  82.9 0.0 copy-start.2
  82.9 0.0 copy-start.6
  82.9 10.0 %all-to-all-start.2 = ((bf16[64,8,640]{2,1,0:T(8,128)(2,1)}), bf16[64,8,640]{2,1,0:T(8,128)(2,1)S(1)}, u32[]{:S(2)}, u32[]{:S(2)}) async-start(bf16[64,8,640]{2,1,0:T(8,128)(2,1)} %bitcast.8), calls=%async_computation.2 | async-start | bytes 1310720 | tf_op jit(solution)/shard_map/all_to_all | solution.py:650
  92.9 0.0 copy-done.1
  92.9 0.0 copy-done.2
  93.0 0.0 copy-done.6
  93.0 0.0 copy-start.7
  93.0 1.2 copy-done.7
  94.2 8.1 %scatter.1 = (f32[2048,512]{1,0:T(8,128)}, f32[8,8,512]{2,1,0:T(8,128)S(1)}) custom-call(f32[512,512]{1,0:T(8,128)S(1)} %copy-done.7, bf16[1024,512]{1,0:T(8,128)(2,1)S(1)} %bitcast.22, s32[1,512]{1,0:T(1,128)S(1)} %get-tuple-element.45.pos_ref, s32[1,512]{1,0:T(1,128)S(1)} %bitcast.24, bf16[1024,512]{1,0:T(8,128)(2,1)S(1)} %copy-done.6, ...), custom_call_target="tpu_custom_call" | custom-call | flops 7000000000 | bytes 10485760 | tf_op jit(solution)/shard_map/scatter/pallas_call | solution.py:490
  102.3 4.4 %all-to-all-done.2 = bf16[64,8,640]{2,1,0:T(8,128)(2,1)S(1)} async-done(((bf16[64,8,640]{2,1,0:T(8,128)(2,1)}), bf16[64,8,640]{2,1,0:T(8,128)(2,1)S(1)}, u32[]{:S(2)}, u32[]{:S(2)}) %all-to-all-start.2) | async-done | bytes 655392 | tf_op jit(solution)/shard_map/all_to_all | solution.py:650
  106.6 0.3 total_up.1
  106.9 18.3 %all_to_all.21 = bf16[64,8,640]{2,1,0:T(8,128)(2,1)S(1)} all-to-all(bf16[64,8,640]{2,1,0:T(8,128)(2,1)S(1)} %bitcast.20), channel_id=1, replica_groups=mesh['z'=4,'y'=4,'c'=2,'x'=4] {'z','y','x'}, dimensions={0} | all-to-all | bytes 1310720 | tf_op jit(solution)/shard_map/all_to_all | solution.py:650
  125.2 2.5 %collective-permute-start.5 = (bf16[512,640]{1,0:T(8,128)(2,1)S(1)}, bf16[512,640]{1,0:T(8,128)(2,1)S(1)}, u32[]{:S(2)}, u32[]{:S(2)}) collective-permute-start(bf16[512,640]{1,0:T(8,128)(2,1)S(1)} %bitcast.17), channel_id=1, source_target_pairs={{0,4},{4,0},{1,5},{5,1},{2,6},{6,2},{3,7},{7,3},{8,12},{12,8},{9,1... | collective-permute-start | bytes 1966088 | tf_op jit(solution)/shard_map/ppermute | solution.py:655
  127.7 2.4 %finish_own.1 = (f32[512,512]{1,0:T(8,128)}, f32[512,512]{1,0:T(8,128)}, f32[1,512]{1,0:T(1,128)}, f32[1,128]{1,0:T(1,128)}, f32[2048,512]{1,0:T(8,128)}) custom-call(bf16[512,640]{1,0:T(8,128)(2,1)S(1)} %bitcast.18, s32[8]{0:T(128)S(1)} %copy-done.2, f32[8,8,512]{2,1,0:T(8,128)S(1)} %get-tuple-element.50.near_ref, ...), custom_call_target="tpu_custom_call", output_to_operand_aliasing={{4}: (3, {})} | custom-call | flops 1000000 | bytes 2097152 | tf_op jit(solution)/shard_map/finish_own/pallas_call | solution.py:602
  130.1 0.0 collective-permute-done.5.other_ref
  130.1 1.1 finish_other.1
  (3 shorter events, 0.0 us)
Async XLA Ops:
  4.6 37.9 %copy-start = (bf16[2048,512]{1,0:T(8,128)(2,1)S(1)}, bf16[2048,512]{1,0:T(8,128)(2,1)}, u32[]{:S(2)}) copy-start(bf16[2048,512]{1,0:T(8,128)(2,1)} %emb_ref.1) | copy-start | bytes 6291460
  38.3 0.7 copy-start.8
  38.3 4.2 %copy-start.3 = (s32[128]{0:T(128)S(1)}, s32[128]{0:T(128)}, u32[]{:S(2)}) copy-start(s32[128]{0:T(128)} %param.16) | copy-start | bytes 1540
  38.5 1.2 collective-permute-start
  39.7 16.3 %collective-permute-start.1 = (f32[8,512]{1,0:T(8,128)S(1)}, f32[8,512]{1,0:T(8,128)S(1)}, u32[]{:S(2)}, u32[]{:S(2)}) collective-permute-start(f32[8,512]{1,0:T(8,128)S(1)} %add.12), channel_id=1, source_target_pairs={{0,1},{1,2},{2,3},{3,0},{4,5},{5,6},{6,7},{7,4},{8,9},{9,10},{10,1... | collective-permute-start | bytes 49160 | tf_op jit(solution)/shard_map/ppermute | solution.py:660
  40.0 16.0 %collective-permute-start.2 = (f32[8,512]{1,0:T(8,128)S(1)}, f32[8,512]{1,0:T(8,128)S(1)}, u32[]{:S(2)}, u32[]{:S(2)}) collective-permute-start(f32[8,512]{1,0:T(8,128)S(1)} %add.12), channel_id=1, source_target_pairs={{0,2},{1,3},{2,0},{3,1},{4,6},{5,7},{6,4},{7,5},{8,10},{9,11},{10,... | collective-permute-start | bytes 49160 | tf_op jit(solution)/shard_map/ppermute | solution.py:660
  42.1 14.0 %collective-permute-start.3 = (f32[8,512]{1,0:T(8,128)S(1)}, f32[8,512]{1,0:T(8,128)S(1)}, u32[]{:S(2)}, u32[]{:S(2)}) collective-permute-start(f32[8,512]{1,0:T(8,128)S(1)} %add.12), channel_id=1, source_target_pairs={{0,3},{1,0},{2,1},{3,2},{4,7},{5,4},{6,5},{7,6},{8,11},{9,8},{10,9... | collective-permute-start | bytes 49160 | tf_op jit(solution)/shard_map/ppermute | solution.py:660
  50.3 5.7 %copy-start.4 = (bf16[512,512]{1,0:T(8,128)(2,1)S(1)}, bf16[512,512]{1,0:T(8,128)(2,1)}, u32[]{:S(2)}) copy-start(bf16[512,512]{1,0:T(8,128)(2,1)} %w1_ref.1) | copy-start | bytes 1572868
  50.3 5.7 %copy-start.5 = (bf16[512,512]{1,0:T(8,128)(2,1)S(1)}, bf16[512,512]{1,0:T(8,128)(2,1)}, u32[]{:S(2)}) copy-start(bf16[512,512]{1,0:T(8,128)(2,1)} %w2_ref.1) | copy-start | bytes 1572868
  50.4 26.7 %all-to-all-start.1 = ((bf16[128,8,512]{2,1,0:T(8,128)(2,1)}), bf16[128,8,512]{2,1,0:T(8,128)(2,1)S(1)}, u32[]{:S(2)}, u32[]{:S(2)}) async-start(bf16[128,8,512]{2,1,0:T(8,128)(2,1)} %bitcast.6), calls=%async_computation.1 | async-start | bytes 2097152 | tf_op jit(solution)/shard_map/all_to_all | solution.py:650
  77.1 3.7 %collective-permute-start.4 = (f32[528,512]{1,0:T(8,128)S(1)}, f32[528,512]{1,0:T(8,128)S(1)}, u32[]{:S(2)}, u32[]{:S(2)}) collective-permute-start(f32[528,512]{1,0:T(8,128)S(1)} %get-tuple-element.41), channel_id=1, source_target_pairs={{0,4},{4,0},{1,5},{5,1},{2,6},{6,2},{3,7},{7,3},{8,12},{12,8},{9,1... | collective-permute-start | bytes 3244040 | tf_op jit(solution)/shard_map/ppermute | solution.py:655
  82.8 10.1 %copy-start.1 = (s32[512]{0:T(512)S(1)}, s32[512]{0:T(512)}, u32[]{:S(2)}) copy-start(s32[512]{0:T(512)} %param.13) | copy-start | bytes 6148
  82.9 10.1 %copy-start.2 = (s32[8]{0:T(128)S(1)}, s32[8]{0:T(128)}, u32[]{:S(2)}) copy-start(s32[8]{0:T(128)} %neg_ref.3) | copy-start | bytes 100
  82.9 10.1 %copy-start.6 = (bf16[1024,512]{1,0:T(8,128)(2,1)S(1)}, bf16[1024,512]{1,0:T(8,128)(2,1)}, u32[]{:S(2)}) copy-start(bf16[1024,512]{1,0:T(8,128)(2,1)} %get-tuple-element.46.gdst_ref) | copy-start | bytes 3145732
  82.9 23.7 %all-to-all-start.2 = ((bf16[64,8,640]{2,1,0:T(8,128)(2,1)}), bf16[64,8,640]{2,1,0:T(8,128)(2,1)S(1)}, u32[]{:S(2)}, u32[]{:S(2)}) async-start(bf16[64,8,640]{2,1,0:T(8,128)(2,1)} %bitcast.8), calls=%async_computation.2 | async-start | bytes 1310720 | tf_op jit(solution)/shard_map/all_to_all | solution.py:650
  93.0 1.2 copy-start.7
  125.2 4.9 %collective-permute-start.5 = (bf16[512,640]{1,0:T(8,128)(2,1)S(1)}, bf16[512,640]{1,0:T(8,128)(2,1)S(1)}, u32[]{:S(2)}, u32[]{:S(2)}) collective-permute-start(bf16[512,640]{1,0:T(8,128)(2,1)S(1)} %bitcast.17), channel_id=1, source_target_pairs={{0,4},{4,0},{1,5},{5,1},{2,6},{6,2},{3,7},{7,3},{8,12},{12,8},{9,1... | collective-permute-start | bytes 1966088 | tf_op jit(solution)/shard_map/ppermute | solution.py:655

commit v3 on v2

--- a/solution.py
+++ b/solution.py
@@ -655,10 +655,8 @@
     return lax.ppermute(rows, "c", [(0, 1), (1, 0)])
 
 
-def complete(rows):
-    rows = rows + swap(rows)
-    got = [lax.ppermute(rows, "x", [(i, (i + by) % 4) for i in range(4)]) for by in (1, 2, 3)]
-    return (rows + got[0]) + (got[1] + got[2])
+def flip(rows, by):
+    return lax.ppermute(rows, "x", [(i, i ^ by) for i in range(4)])
 
 
 def body(embeddings, w_first, w_second, w_score, src_row, dst_owner, dst_row, edge_count, neg_ids):
@@ -669,8 +667,13 @@
         embeddings, src_row, dst_owner.reshape(1, EDGES), dst_row.reshape(1, EDGES), ec, neg_ids
     )
     recv = exchange(push, AXES)
-    negs = complete(pick(recv))
+    negs = pick(recv)
+    negs = negs + swap(negs)
+    near_x = flip(negs, 1)
     ret, gdst, rows, g1, g2, gs, loss = positive(recv, embeddings, w_first, w_second, ws, ec)
+    ret, near_x = lax.optimization_barrier((ret, near_x))
+    negs = negs + near_x
+    negs = negs + flip(negs, 2)
     back = exchange(ret, AXES)
     keep, send, gsrc, extra = negative(semb, negs, w_first, w_second, ws, ec, g1, g2, gs, loss)
     send, back = lax.optimization_barrier((send, back))

time: 132 us -> 133 us (level); the launches traced: 131 us -> 134 us
  starting transfers between devices: 22.6 us -> 25.5 us
    all_to_all x2, starting transfers between devices: 15.7 us -> 18.9 us  [exchange(): out = lax.all_to_all(parts, axes, split_axis=0, concat_axis=0, tiled=True)]
    ppermute x3 -> x2, starting transfers between devices: 2.76 us -> 2.4 us  [flip(): return lax.ppermute(rows, 'x', [(i, i ^ by) for i in range(4)])]
  transfers between devices with their start and end apart: 8 -> 7, of which waited for: 3 -> 3; matrix products, arithmetic and copies ran while one was open for 0% -> 0% of each run, Pallas kernels for 30% -> 29%
where the time goes in v3:
time: 133 us; the launch traced here: 134 us
  blocking collectives  51.9 us (39%)
  Pallas kernels  46.9 us (35%)
  starting transfers between devices  25.5 us (19%)
  waiting for transfers between devices  7.42 us (6%)
  local copies, waits for them, and re-layouts  1.33 us (1%)
    all_to_all x2, blocking collectives, exchange(): out = lax.all_to_all(parts, axes, split_axis=0, concat_axis=0, tiled=True)  51.9 us
    pallas_call x1, Pallas kernels, negative(): pl.pallas_call(negative_kernel, in_specs=[HBM] + [VMEM] * 5 + [HBM] * 2 +...  21 us
    all_to_all x2, starting transfers between devices, exchange(): out = lax.all_to_all(parts, axes, split_axis=0, concat_axis=0, tiled=True)  18.9 us
    pallas_call x1, Pallas kernels, scatter(): pl.pallas_call(scatter_kernel, grid=(ROWS // block,), in_specs=[whole((ED...  8.11 us
    pallas_call x1, Pallas kernels, positive(): pl.pallas_call(positive_kernel, in_specs=[VMEM, VMEM, HBM, HBM, VMEM, VME...  7.79 us
    all_to_all x2, waiting for transfers between devices, exchange(): out = lax.all_to_all(parts, axes, split_axis=0, concat_axis=0, tiled=True)  4.3 us
    ppermute x3, starting transfers between devices, swap(): return lax.ppermute(rows, 'c', [(0, 1), (1, 0)])  4.23 us
    pallas_call x1, Pallas kernels, prepare(): pl.pallas_call(prepare_kernel, in_specs=[HBM] * 6, out_specs=[VMEM, HBM,...  3.93 us
  transfers between devices with their start and end apart: 7, of which 3 were waited for; matrix products, arithmetic and copies ran while one was open for 0% of the time, Pallas kernels for 29%

profile of v3, /device:TPU:1, one launch (start us, length us, event | category | flops | bytes accessed | tf_op | source)
XLA Modules:
  0.0 134.1 jit_solution(14130349759971178982)
XLA Ops:
  0.6 3.9 %prepare.1 = (bf16[1024,640]{1,0:T(8,128)(2,1)S(1)}, bf16[512,512]{1,0:T(8,128)(2,1)}, s32[1,512]{1,0:T(1,128)S(1)}) custom-call(bf16[2048,512]{1,0:T(8,128)(2,1)} %emb_ref.1, s32[1,512]{1,0:T(1,128)} %bitcast.23, s32[1,512]{1,0:T(1,128)} %bitcast.28, s32[1,512]{1,0:T(1,128)} %bitcast.29, s32[1,128]{1,0:T(1,128)} %bitcast.25, s32[8]{0:T(128)} %neg_ref.3), custom_call_target="tpu_custom_call" | custom-call | tf_op jit(solution)/shard_map/prepare/pallas_call | solution.py:141
  4.6 0.0 copy-start
  4.6 33.7 %all_to_all.20 = bf16[128,8,640]{2,1,0:T(8,128)(2,1)S(1)} all-to-all(bf16[128,8,640]{2,1,0:T(8,128)(2,1)S(1)} %bitcast.21), channel_id=1, replica_groups=mesh['z'=4,'y'=4,'c'=2,'x'=4] {'z','y','c','x'}, dimensions={0} | all-to-all | bytes 2621440 | tf_op jit(solution)/shard_map/all_to_all | solution.py:650
  38.3 0.0 copy-start.8
  38.3 0.0 copy-start.3
  38.3 0.2 pick.1
  38.5 0.4 collective-permute-start
  38.9 0.1 copy-done.8
  39.0 0.8 collective-permute-done
  39.7 0.3 collective-permute-start.1
  40.0 0.0 copy-done
  40.1 0.0 copy-done.3
  40.1 7.8 %positive.1 = (bf16[1024,512]{1,0:T(8,128)(2,1)}, bf16[1024,512]{1,0:T(8,128)(2,1)}, f32[8,1024]{1,0:T(8,128)S(1)}, f32[512,512]{1,0:T(8,128)}, f32[512,512]{1,0...) custom-call(bf16[1024,640]{1,0:T(8,128)(2,1)S(1)} %bitcast.16, bf16[2048,512]{1,0:T(8,128)(2,1)S(1)} %copy-done, ...), custom_call_target="tpu_custom_call" | custom-call | flops 6000000000 | bytes 12582912 | tf_op jit(solution)/shard_map/positive/pallas_call | solution.py:302
  47.9 0.0 copy-start.4
  47.9 0.0 copy-start.5
  47.9 0.0 collective-permute-done.1
  47.9 2.1 %collective-permute-start.2 = (f32[8,512]{1,0:T(8,128)S(1)}, f32[8,512]{1,0:T(8,128)S(1)}, u32[]{:S(2)}, u32[]{:S(2)}) collective-permute-start(f32[8,512]{1,0:T(8,128)S(1)} %add.10), channel_id=1, source_target_pairs={{0,2},{1,3},{2,0},{3,1},{4,6},{5,7},{6,4},{7,5},{8,10},{9,11},{10,... | collective-permute-start | bytes 49160 | tf_op jit(solution)/shard_map/ppermute | solution.py:659
  50.0 8.9 %all-to-all-start.1 = ((bf16[128,8,512]{2,1,0:T(8,128)(2,1)}), bf16[128,8,512]{2,1,0:T(8,128)(2,1)S(1)}, u32[]{:S(2)}, u32[]{:S(2)}) async-start(bf16[128,8,512]{2,1,0:T(8,128)(2,1)} %bitcast.6), calls=%async_computation.1 | async-start | bytes 2097152 | tf_op jit(solution)/shard_map/all_to_all | solution.py:650
  58.9 0.0 collective-permute-done.2
  58.9 0.0 copy-done.4
  58.9 0.0 copy-done.5
  58.9 21.0 %negative.1 = (f32[512,512]{1,0:T(8,128)}, f32[528,512]{1,0:T(8,128)S(1)}, f32[512,512]{1,0:T(8,128)}, f32[16,512]{1,0:T(8,128)S(1)}) custom-call(bf16[512,512]{1,0:T(8,128)(2,1)} %get-tuple-element.34.semb_hbm, f32[8,512]{1,0:T(8,128)S(1)} %add.11.neg_ref, bf16[512,512]{1,0:T(8,128)(2,1)S(1)} %copy-done.4, bf16[512,512]{1,0:T(8,128)(2,1)S(1)} %copy-done.5, ...), custom_call_target="tpu_custom_call" | custom-call | flops 20000000000 | bytes 8388608 | tf_op jit(solution)/shard_map/negative/pallas_call | solution.py:401
  79.9 0.0 all-to-all-done.1
  79.9 1.3 collective-permute-start.3
  81.2 2.3 %collective-permute-done.3.got_ref = f32[528,512]{1,0:T(8,128)S(1)} collective-permute-done((f32[528,512]{1,0:T(8,128)S(1)}, f32[528,512]{1,0:T(8,128)S(1)}, u32[]{:S(2)}, u32[]{:S(2)}) %collective-permute-start.3) | collective-permute-done | bytes 1081376 | tf_op jit(solution)/shard_map/ppermute | solution.py:655
  83.6 2.1 %join.1 = bf16[512,640]{1,0:T(8,128)(2,1)} custom-call(f32[512,512]{1,0:T(8,128)} %get-tuple-element.42.keep_hbm, f32[528,512]{1,0:T(8,128)S(1)} %collective-permute-done.3.got_ref, f32[16,512]{1,0:T(8,128)S(1)} %get-tuple-element.46.mine_ref), custom_call_target="tpu_custom_call" | custom-call | tf_op jit(solution)/shard_map/join/pallas_call | solution.py:446
  85.7 0.0 copy-start.1
  85.7 0.0 copy-start.2
  85.7 0.0 copy-start.6
  85.7 10.0 %all-to-all-start.2 = ((bf16[64,8,640]{2,1,0:T(8,128)(2,1)}), bf16[64,8,640]{2,1,0:T(8,128)(2,1)S(1)}, u32[]{:S(2)}, u32[]{:S(2)}) async-start(bf16[64,8,640]{2,1,0:T(8,128)(2,1)} %bitcast.8), calls=%async_computation.2 | async-start | bytes 1310720 | tf_op jit(solution)/shard_map/all_to_all | solution.py:650
  95.8 0.0 copy-done.1
  95.8 0.0 copy-done.2
  95.8 0.0 copy-done.6
  95.8 0.0 copy-start.7
  95.8 1.2 copy-done.7
  97.0 8.1 %scatter.1 = (f32[2048,512]{1,0:T(8,128)}, f32[8,8,512]{2,1,0:T(8,128)S(1)}) custom-call(f32[512,512]{1,0:T(8,128)S(1)} %copy-done.7, bf16[1024,512]{1,0:T(8,128)(2,1)S(1)} %bitcast.22, s32[1,512]{1,0:T(1,128)S(1)} %get-tuple-element.49.pos_ref, s32[1,512]{1,0:T(1,128)S(1)} %bitcast.24, bf16[1024,512]{1,0:T(8,128)(2,1)S(1)} %copy-done.6, ...), custom_call_target="tpu_custom_call" | custom-call | flops 7000000000 | bytes 10485760 | tf_op jit(solution)/shard_map/scatter/pallas_call | solution.py:490
  105.1 4.3 %all-to-all-done.2 = bf16[64,8,640]{2,1,0:T(8,128)(2,1)S(1)} async-done(((bf16[64,8,640]{2,1,0:T(8,128)(2,1)}), bf16[64,8,640]{2,1,0:T(8,128)(2,1)S(1)}, u32[]{:S(2)}, u32[]{:S(2)}) %all-to-all-start.2) | async-done | bytes 655392 | tf_op jit(solution)/shard_map/all_to_all | solution.py:650
  109.4 0.3 total_up.1
  109.7 18.2 %all_to_all.21 = bf16[64,8,640]{2,1,0:T(8,128)(2,1)S(1)} all-to-all(bf16[64,8,640]{2,1,0:T(8,128)(2,1)S(1)} %bitcast.20), channel_id=1, replica_groups=mesh['z'=4,'y'=4,'c'=2,'x'=4] {'z','y','x'}, dimensions={0} | all-to-all | bytes 1310720 | tf_op jit(solution)/shard_map/all_to_all | solution.py:650
  127.9 2.5 %collective-permute-start.4 = (bf16[512,640]{1,0:T(8,128)(2,1)S(1)}, bf16[512,640]{1,0:T(8,128)(2,1)S(1)}, u32[]{:S(2)}, u32[]{:S(2)}) collective-permute-start(bf16[512,640]{1,0:T(8,128)(2,1)S(1)} %bitcast.17), channel_id=1, source_target_pairs={{0,4},{4,0},{1,5},{5,1},{2,6},{6,2},{3,7},{7,3},{8,12},{12,8},{9,1... | collective-permute-start | bytes 1966088 | tf_op jit(solution)/shard_map/ppermute | solution.py:655
  130.4 2.4 %finish_own.1 = (f32[512,512]{1,0:T(8,128)}, f32[512,512]{1,0:T(8,128)}, f32[1,512]{1,0:T(1,128)}, f32[1,128]{1,0:T(1,128)}, f32[2048,512]{1,0:T(8,128)}) custom-call(bf16[512,640]{1,0:T(8,128)(2,1)S(1)} %bitcast.18, s32[8]{0:T(128)S(1)} %copy-done.2, f32[8,8,512]{2,1,0:T(8,128)S(1)} %get-tuple-element.54.near_ref, ...), custom_call_target="tpu_custom_call", output_to_operand_aliasing={{4}: (3, {})} | custom-call | flops 1000000 | bytes 2097152 | tf_op jit(solution)/shard_map/finish_own/pallas_call | solution.py:602
  132.9 0.0 collective-permute-done.4.other_ref
  132.9 1.1 finish_other.1
  (4 shorter events, 0.0 us)
Async XLA Ops:
  4.6 35.5 %copy-start = (bf16[2048,512]{1,0:T(8,128)(2,1)S(1)}, bf16[2048,512]{1,0:T(8,128)(2,1)}, u32[]{:S(2)}) copy-start(bf16[2048,512]{1,0:T(8,128)(2,1)} %emb_ref.1) | copy-start | bytes 6291460
  38.3 0.7 copy-start.8
  38.3 1.8 %copy-start.3 = (s32[128]{0:T(128)S(1)}, s32[128]{0:T(128)}, u32[]{:S(2)}) copy-start(s32[128]{0:T(128)} %param.16) | copy-start | bytes 1540
  38.5 1.2 collective-permute-start
  39.7 8.1 %collective-permute-start.1 = (f32[8,512]{1,0:T(8,128)S(1)}, f32[8,512]{1,0:T(8,128)S(1)}, u32[]{:S(2)}, u32[]{:S(2)}) collective-permute-start(f32[8,512]{1,0:T(8,128)S(1)} %add.9), channel_id=1, source_target_pairs={{0,1},{1,0},{2,3},{3,2},{4,5},{5,4},{6,7},{7,6},{8,9},{9,8},{10,11... | collective-permute-start | bytes 49160 | tf_op jit(solution)/shard_map/ppermute | solution.py:659
  47.9 11.0 %copy-start.4 = (bf16[512,512]{1,0:T(8,128)(2,1)S(1)}, bf16[512,512]{1,0:T(8,128)(2,1)}, u32[]{:S(2)}) copy-start(bf16[512,512]{1,0:T(8,128)(2,1)} %w1_ref.1) | copy-start | bytes 1572868
  47.9 11.0 %copy-start.5 = (bf16[512,512]{1,0:T(8,128)(2,1)S(1)}, bf16[512,512]{1,0:T(8,128)(2,1)}, u32[]{:S(2)}) copy-start(bf16[512,512]{1,0:T(8,128)(2,1)} %w2_ref.1) | copy-start | bytes 1572868
  47.9 11.0 %collective-permute-start.2 = (f32[8,512]{1,0:T(8,128)S(1)}, f32[8,512]{1,0:T(8,128)S(1)}, u32[]{:S(2)}, u32[]{:S(2)}) collective-permute-start(f32[8,512]{1,0:T(8,128)S(1)} %add.10), channel_id=1, source_target_pairs={{0,2},{1,3},{2,0},{3,1},{4,6},{5,7},{6,4},{7,5},{8,10},{9,11},{10,... | collective-permute-start | bytes 49160 | tf_op jit(solution)/shard_map/ppermute | solution.py:659
  50.0 29.9 %all-to-all-start.1 = ((bf16[128,8,512]{2,1,0:T(8,128)(2,1)}), bf16[128,8,512]{2,1,0:T(8,128)(2,1)S(1)}, u32[]{:S(2)}, u32[]{:S(2)}) async-start(bf16[128,8,512]{2,1,0:T(8,128)(2,1)} %bitcast.6), calls=%async_computation.1 | async-start | bytes 2097152 | tf_op jit(solution)/shard_map/all_to_all | solution.py:650
  79.9 3.7 %collective-permute-start.3 = (f32[528,512]{1,0:T(8,128)S(1)}, f32[528,512]{1,0:T(8,128)S(1)}, u32[]{:S(2)}, u32[]{:S(2)}) collective-permute-start(f32[528,512]{1,0:T(8,128)S(1)} %get-tuple-element.45), channel_id=1, source_target_pairs={{0,4},{4,0},{1,5},{5,1},{2,6},{6,2},{3,7},{7,3},{8,12},{12,8},{9,1... | collective-permute-start | bytes 3244040 | tf_op jit(solution)/shard_map/ppermute | solution.py:655
  85.7 10.1 %copy-start.1 = (s32[512]{0:T(512)S(1)}, s32[512]{0:T(512)}, u32[]{:S(2)}) copy-start(s32[512]{0:T(512)} %param.13) | copy-start | bytes 6148
  85.7 10.1 %copy-start.2 = (s32[8]{0:T(128)S(1)}, s32[8]{0:T(128)}, u32[]{:S(2)}) copy-start(s32[8]{0:T(128)} %neg_ref.3) | copy-start | bytes 100
  85.7 10.1 %copy-start.6 = (bf16[1024,512]{1,0:T(8,128)(2,1)S(1)}, bf16[1024,512]{1,0:T(8,128)(2,1)}, u32[]{:S(2)}) copy-start(bf16[1024,512]{1,0:T(8,128)(2,1)} %get-tuple-element.50.gdst_ref) | copy-start | bytes 3145732
  85.7 23.7 %all-to-all-start.2 = ((bf16[64,8,640]{2,1,0:T(8,128)(2,1)}), bf16[64,8,640]{2,1,0:T(8,128)(2,1)S(1)}, u32[]{:S(2)}, u32[]{:S(2)}) async-start(bf16[64,8,640]{2,1,0:T(8,128)(2,1)} %bitcast.8), calls=%async_computation.2 | async-start | bytes 1310720 | tf_op jit(solution)/shard_map/all_to_all | solution.py:650
  95.8 1.2 copy-start.7
  127.9 4.9 %collective-permute-start.4 = (bf16[512,640]{1,0:T(8,128)(2,1)S(1)}, bf16[512,640]{1,0:T(8,128)(2,1)S(1)}, u32[]{:S(2)}, u32[]{:S(2)}) collective-permute-start(bf16[512,640]{1,0:T(8,128)(2,1)S(1)} %bitcast.17), channel_id=1, source_target_pairs={{0,4},{4,0},{1,5},{5,1},{2,6},{6,2},{3,7},{7,3},{8,12},{12,8},{9,1... | collective-permute-start | bytes 1966088 | tf_op jit(solution)/shard_map/ppermute | solution.py:655

commit v4 on v3

--- a/solution.py
+++ b/solution.py
@@ -248,7 +248,6 @@
     half = SLOTS // 2
     rounds = jnp.where(jnp.sum(taken) > half, 2, 1)
     row_ref[...] = jnp.full(row_ref.shape, -1.0, F32)
-    ret_ref[...] = jnp.zeros_like(ret_ref)
 
     def step(h, carry):
         rows = pl.ds(pl.multiple_of(h * half, half), half)
@@ -290,7 +289,15 @@
         gdst_ref[rows, :] = (dx * src).astype(BF16)
         outs[2].start()
         back = mm(onehot_rows(place_col - h * half, half), (dx * dst).astype(BF16))
-        ret_ref[...] = (ret_ref[...].astype(F32) + back).astype(BF16)
+
+        @pl.when(h == 0)
+        def _():
+            ret_ref[...] = back.astype(BF16)
+
+        @pl.when(h > 0)
+        def _():
+            ret_ref[...] = (ret_ref[...].astype(F32) + back).astype(BF16)
+
         for copy in outs:
             copy.wait()
         return carry
@@ -329,7 +336,7 @@
 
 def negative_kernel(semb_hbm, neg_ref, w1_ref, w2_ref, ws_ref, ec_ref, g1_in, g2_in, gs_in, loss_in,
                     keep_hbm, send_ref, gsrc_hbm, extra_ref, gsrc_ref, g1_ref, g2_ref, gs_ref, loss_ref, gneg_ref,
-                    semb_ref, sems):
+                    semb_ref, sems, out_sems):
     core = lax.axis_index("c")
     first = pltpu.make_async_copy(semb_hbm, semb_ref, sems.at[4])
     first.start()
@@ -374,16 +381,26 @@
                     pltpu.make_async_copy(kept, keep_hbm, sems.at[3]).start()
 
         dxs = decode_parts(xs, [head] * 4, w1, w2, wsb, wsr, g1_ref, g2_ref, ready, summed)
-        gsrc = gsrc_ref[...]
-        for k, n, dx in zip(ks, negs, dxs):
-            gsrc = gsrc + dx * n
+        for q in range(4):
+            rows = slice(q * 128, q * 128 + 128)
+            gsrc = gsrc_ref[rows, :]
+            for n, dx in zip(negs, dxs):
+                gsrc = gsrc + dx[rows, :] * n
+            gsrc_ref[rows, :] = gsrc
+
+            @pl.when(i == NEG // 4 - 1)
+            def _():
+                outs[q].start()
+
+        for k, dx in zip(ks, dxs):
             gneg_ref[pl.ds(k, 1), :] = jnp.sum(dx * src, axis=0, keepdims=True)
-        gsrc_ref[...] = gsrc
         return carry
 
+    outs = []
+    for q in range(4):
+        rows = pl.ds(q * 128, 128)
+        outs.append(pltpu.make_async_copy(gsrc_ref.at[rows, :], gsrc_hbm.at[rows, :], out_sems.at[q]))
     lax.fori_loop(0, NEG // 4, step, 0)
-    out = pltpu.make_async_copy(gsrc_ref, gsrc_hbm, sems.at[2])
-    out.start()
     loss = jnp.concatenate([loss_ref[...], jnp.zeros((1, WIDTH - LANES), F32)], axis=1)
     extra = jnp.concatenate([gneg_ref[...] * 2.0, gs_ref[...], loss, jnp.zeros((6, WIDTH), F32)], axis=0)
     extra_ref[...] = extra
@@ -394,7 +411,8 @@
             send_ref[0:WIDTH, :] = sent[...]
             pltpu.make_async_copy(kept, keep_hbm, sems.at[3]).wait()
 
-    out.wait()
+    for out in outs:
+        out.wait()
 
 
 def negative(semb, negs, w1, w2, ws, ec, g1, g2, gs, loss):
@@ -414,6 +432,7 @@
             pltpu.VMEM((NEG, WIDTH), F32),
             pltpu.VMEM((EDGES, WIDTH), BF16),
             pltpu.SemaphoreType.DMA((5,)),
+            pltpu.SemaphoreType.DMA((4,)),
         ],
         compiler_params=pltpu.CompilerParams(vmem_limit_bytes=40 * MIB),
         cost_estimate=pl.CostEstimate(flops=20_000_000_000, bytes_accessed=8 * MIB, transcendentals=0),

time: 133 us -> 130 us (0.977); the launches traced: 134 us -> 130 us
  starting transfers between devices: 25.5 us -> 21.3 us
    all_to_all x2, starting transfers between devices: 18.9 us -> 14.7 us  [exchange(): out = lax.all_to_all(parts, axes, split_axis=0, concat_axis=0, tiled=True)]
  transfers between devices with their start and end apart: 7 -> 7, of which waited for: 3 -> 3; matrix products, arithmetic and copies ran while one was open for 0% -> 0% of each run, Pallas kernels for 29% -> 30%
where the time goes in v4:
time: 130 us
  blocking collectives  51.9 us (40%)
  Pallas kernels  46.8 us (36%)
  starting transfers between devices  21.3 us (16%)
  waiting for transfers between devices  7.4 us (6%)
  local copies, waits for them, and re-layouts  1.33 us (1%)
    all_to_all x2, blocking collectives, exchange(): out = lax.all_to_all(parts, axes, split_axis=0, concat_axis=0, tiled=True)  51.9 us
    pallas_call x1, Pallas kernels, negative(): pl.pallas_call(negative_kernel, in_specs=[HBM] + [VMEM] * 5 + [HBM] * 2 +...  20.9 us
    all_to_all x2, starting transfers between devices, exchange(): out = lax.all_to_all(parts, axes, split_axis=0, concat_axis=0, tiled=True)  14.7 us
    pallas_call x1, Pallas kernels, scatter(): pl.pallas_call(scatter_kernel, grid=(ROWS // block,), in_specs=[whole((ED...  8.13 us
    pallas_call x1, Pallas kernels, positive(): pl.pallas_call(positive_kernel, in_specs=[VMEM, VMEM, HBM, HBM, VMEM, VME...  7.73 us
    all_to_all x2, waiting for transfers between devices, exchange(): out = lax.all_to_all(parts, axes, split_axis=0, concat_axis=0, tiled=True)  4.29 us
    ppermute x3, starting transfers between devices, swap(): return lax.ppermute(rows, 'c', [(0, 1), (1, 0)])  4.23 us
    pallas_call x1, Pallas kernels, prepare(): pl.pallas_call(prepare_kernel, in_specs=[HBM] * 6, out_specs=[VMEM, HBM,...  3.93 us
  transfers between devices with their start and end apart: 7, of which 3 were waited for; matrix products, arithmetic and copies ran while one was open for 0% of the time, Pallas kernels for 30%

profile of v4, /device:TPU:1, one launch (start us, length us, event | category | flops | bytes accessed | tf_op | source)
XLA Modules:
  0.0 129.8 jit_solution(14403499330577409090)
XLA Ops:
  0.6 3.9 %prepare.1 = (bf16[1024,640]{1,0:T(8,128)(2,1)S(1)}, bf16[512,512]{1,0:T(8,128)(2,1)}, s32[1,512]{1,0:T(1,128)S(1)}) custom-call(bf16[2048,512]{1,0:T(8,128)(2,1)} %emb_ref.1, s32[1,512]{1,0:T(1,128)} %bitcast.23, s32[1,512]{1,0:T(1,128)} %bitcast.28, s32[1,512]{1,0:T(1,128)} %bitcast.29, s32[1,128]{1,0:T(1,128)} %bitcast.25, s32[8]{0:T(128)} %neg_ref.3), custom_call_target="tpu_custom_call" | custom-call | tf_op jit(solution)/shard_map/prepare/pallas_call | solution.py:141
  4.6 0.0 copy-start
  4.6 33.7 %all_to_all.20 = bf16[128,8,640]{2,1,0:T(8,128)(2,1)S(1)} all-to-all(bf16[128,8,640]{2,1,0:T(8,128)(2,1)S(1)} %bitcast.21), channel_id=1, replica_groups=mesh['z'=4,'y'=4,'c'=2,'x'=4] {'z','y','c','x'}, dimensions={0} | all-to-all | bytes 2621440 | tf_op jit(solution)/shard_map/all_to_all | solution.py:669
  38.3 0.0 copy-start.8
  38.3 0.0 copy-start.3
  38.3 0.2 pick.1
  38.5 0.4 collective-permute-start
  38.9 0.1 copy-done.8
  39.0 0.8 collective-permute-done
  39.7 0.3 collective-permute-start.1
  40.0 0.0 copy-done
  40.1 0.0 copy-done.3
  40.1 7.7 %positive.1 = (bf16[1024,512]{1,0:T(8,128)(2,1)}, bf16[1024,512]{1,0:T(8,128)(2,1)}, f32[8,1024]{1,0:T(8,128)S(1)}, f32[512,512]{1,0:T(8,128)}, f32[512,512]{1,0...) custom-call(bf16[1024,640]{1,0:T(8,128)(2,1)S(1)} %bitcast.16, bf16[2048,512]{1,0:T(8,128)(2,1)S(1)} %copy-done, ...), custom_call_target="tpu_custom_call" | custom-call | flops 6000000000 | bytes 12582912 | tf_op jit(solution)/shard_map/positive/pallas_call | solution.py:309
  47.8 0.0 copy-start.4
  47.8 0.0 copy-start.5
  47.8 0.0 collective-permute-done.1
  47.8 2.1 %collective-permute-start.2 = (f32[8,512]{1,0:T(8,128)S(1)}, f32[8,512]{1,0:T(8,128)S(1)}, u32[]{:S(2)}, u32[]{:S(2)}) collective-permute-start(f32[8,512]{1,0:T(8,128)S(1)} %add.10), channel_id=1, source_target_pairs={{0,2},{1,3},{2,0},{3,1},{4,6},{5,7},{6,4},{7,5},{8,10},{9,11},{10,... | collective-permute-start | bytes 49160 | tf_op jit(solution)/shard_map/ppermute | solution.py:678
  49.9 4.7 %all-to-all-start.1 = ((bf16[128,8,512]{2,1,0:T(8,128)(2,1)}), bf16[128,8,512]{2,1,0:T(8,128)(2,1)S(1)}, u32[]{:S(2)}, u32[]{:S(2)}) async-start(bf16[128,8,512]{2,1,0:T(8,128)(2,1)} %bitcast.6), calls=%async_computation.1 | async-start | bytes 2097152 | tf_op jit(solution)/shard_map/all_to_all | solution.py:669
  54.6 0.0 collective-permute-done.2
  54.6 0.0 copy-done.4
  54.6 0.0 copy-done.5
  54.6 20.9 %negative.1 = (f32[512,512]{1,0:T(8,128)}, f32[528,512]{1,0:T(8,128)S(1)}, f32[512,512]{1,0:T(8,128)}, f32[16,512]{1,0:T(8,128)S(1)}) custom-call(bf16[512,512]{1,0:T(8,128)(2,1)} %get-tuple-element.34.semb_hbm, f32[8,512]{1,0:T(8,128)S(1)} %add.11.neg_ref, bf16[512,512]{1,0:T(8,128)(2,1)S(1)} %copy-done.4, bf16[512,512]{1,0:T(8,128)(2,1)S(1)} %copy-done.5, ...), custom_call_target="tpu_custom_call" | custom-call | flops 20000000000 | bytes 8388608 | tf_op jit(solution)/shard_map/negative/pallas_call | solution.py:419
  75.6 0.0 all-to-all-done.1
  75.6 1.3 %collective-permute-start.3 = (f32[528,512]{1,0:T(8,128)S(1)}, f32[528,512]{1,0:T(8,128)S(1)}, u32[]{:S(2)}, u32[]{:S(2)}) collective-permute-start(f32[528,512]{1,0:T(8,128)S(1)} %get-tuple-element.45), channel_id=1, source_target_pairs={{0,4},{4,0},{1,5},{5,1},{2,6},{6,2},{3,7},{7,3},{8,12},{12,8},{9,1... | collective-permute-start | bytes 3244040 | tf_op jit(solution)/shard_map/ppermute | solution.py:674
  76.9 2.3 %collective-permute-done.3.got_ref = f32[528,512]{1,0:T(8,128)S(1)} collective-permute-done((f32[528,512]{1,0:T(8,128)S(1)}, f32[528,512]{1,0:T(8,128)S(1)}, u32[]{:S(2)}, u32[]{:S(2)}) %collective-permute-start.3) | collective-permute-done | bytes 1081376 | tf_op jit(solution)/shard_map/ppermute | solution.py:674
  79.2 2.1 %join.1 = bf16[512,640]{1,0:T(8,128)(2,1)} custom-call(f32[512,512]{1,0:T(8,128)} %get-tuple-element.42.keep_hbm, f32[528,512]{1,0:T(8,128)S(1)} %collective-permute-done.3.got_ref, f32[16,512]{1,0:T(8,128)S(1)} %get-tuple-element.46.mine_ref), custom_call_target="tpu_custom_call" | custom-call | tf_op jit(solution)/shard_map/join/pallas_call | solution.py:465
  81.3 0.0 copy-start.1
  81.3 0.0 copy-start.2
  81.3 0.0 copy-start.6
  81.3 10.0 %all-to-all-start.2 = ((bf16[64,8,640]{2,1,0:T(8,128)(2,1)}), bf16[64,8,640]{2,1,0:T(8,128)(2,1)S(1)}, u32[]{:S(2)}, u32[]{:S(2)}) async-start(bf16[64,8,640]{2,1,0:T(8,128)(2,1)} %bitcast.8), calls=%async_computation.2 | async-start | bytes 1310720 | tf_op jit(solution)/shard_map/all_to_all | solution.py:669
  91.4 0.0 copy-done.1
  91.4 0.0 copy-done.2
  91.4 0.0 copy-done.6
  91.4 0.0 copy-start.7
  91.4 1.2 copy-done.7
  92.7 8.1 %scatter.1 = (f32[2048,512]{1,0:T(8,128)}, f32[8,8,512]{2,1,0:T(8,128)S(1)}) custom-call(f32[512,512]{1,0:T(8,128)S(1)} %copy-done.7, bf16[1024,512]{1,0:T(8,128)(2,1)S(1)} %bitcast.22, s32[1,512]{1,0:T(1,128)S(1)} %get-tuple-element.49.pos_ref, s32[1,512]{1,0:T(1,128)S(1)} %bitcast.24, bf16[1024,512]{1,0:T(8,128)(2,1)S(1)} %copy-done.6, ...), custom_call_target="tpu_custom_call" | custom-call | flops 7000000000 | bytes 10485760 | tf_op jit(solution)/shard_map/scatter/pallas_call | solution.py:509
  100.8 4.3 %all-to-all-done.2 = bf16[64,8,640]{2,1,0:T(8,128)(2,1)S(1)} async-done(((bf16[64,8,640]{2,1,0:T(8,128)(2,1)}), bf16[64,8,640]{2,1,0:T(8,128)(2,1)S(1)}, u32[]{:S(2)}, u32[]{:S(2)}) %all-to-all-start.2) | async-done | bytes 655392 | tf_op jit(solution)/shard_map/all_to_all | solution.py:669
  105.1 0.3 total_up.1
  105.4 18.2 %all_to_all.21 = bf16[64,8,640]{2,1,0:T(8,128)(2,1)S(1)} all-to-all(bf16[64,8,640]{2,1,0:T(8,128)(2,1)S(1)} %bitcast.20), channel_id=1, replica_groups=mesh['z'=4,'y'=4,'c'=2,'x'=4] {'z','y','x'}, dimensions={0} | all-to-all | bytes 1310720 | tf_op jit(solution)/shard_map/all_to_all | solution.py:669
  123.6 2.5 %collective-permute-start.4 = (bf16[512,640]{1,0:T(8,128)(2,1)S(1)}, bf16[512,640]{1,0:T(8,128)(2,1)S(1)}, u32[]{:S(2)}, u32[]{:S(2)}) collective-permute-start(bf16[512,640]{1,0:T(8,128)(2,1)S(1)} %bitcast.17), channel_id=1, source_target_pairs={{0,4},{4,0},{1,5},{5,1},{2,6},{6,2},{3,7},{7,3},{8,12},{12,8},{9,1... | collective-permute-start | bytes 1966088 | tf_op jit(solution)/shard_map/ppermute | solution.py:674
  126.1 2.4 %finish_own.1 = (f32[512,512]{1,0:T(8,128)}, f32[512,512]{1,0:T(8,128)}, f32[1,512]{1,0:T(1,128)}, f32[1,128]{1,0:T(1,128)}, f32[2048,512]{1,0:T(8,128)}) custom-call(bf16[512,640]{1,0:T(8,128)(2,1)S(1)} %bitcast.18, s32[8]{0:T(128)S(1)} %copy-done.2, f32[8,8,512]{2,1,0:T(8,128)S(1)} %get-tuple-element.54.near_ref, ...), custom_call_target="tpu_custom_call", output_to_operand_aliasing={{4}: (3, {})} | custom-call | flops 1000000 | bytes 2097152 | tf_op jit(solution)/shard_map/finish_own/pallas_call | solution.py:621
  128.5 0.0 collective-permute-done.4.other_ref
  128.5 1.1 finish_other.1
  (4 shorter events, 0.0 us)
Async XLA Ops:
  4.6 35.5 %copy-start = (bf16[2048,512]{1,0:T(8,128)(2,1)S(1)}, bf16[2048,512]{1,0:T(8,128)(2,1)}, u32[]{:S(2)}) copy-start(bf16[2048,512]{1,0:T(8,128)(2,1)} %emb_ref.1) | copy-start | bytes 6291460
  38.3 0.7 copy-start.8
  38.3 1.8 %copy-start.3 = (s32[128]{0:T(128)S(1)}, s32[128]{0:T(128)}, u32[]{:S(2)}) copy-start(s32[128]{0:T(128)} %param.16) | copy-start | bytes 1540
  38.5 1.2 collective-permute-start
  39.7 8.1 %collective-permute-start.1 = (f32[8,512]{1,0:T(8,128)S(1)}, f32[8,512]{1,0:T(8,128)S(1)}, u32[]{:S(2)}, u32[]{:S(2)}) collective-permute-start(f32[8,512]{1,0:T(8,128)S(1)} %add.9), channel_id=1, source_target_pairs={{0,1},{1,0},{2,3},{3,2},{4,5},{5,4},{6,7},{7,6},{8,9},{9,8},{10,11... | collective-permute-start | bytes 49160 | tf_op jit(solution)/shard_map/ppermute | solution.py:678
  47.8 6.8 %copy-start.4 = (bf16[512,512]{1,0:T(8,128)(2,1)S(1)}, bf16[512,512]{1,0:T(8,128)(2,1)}, u32[]{:S(2)}) copy-start(bf16[512,512]{1,0:T(8,128)(2,1)} %w1_ref.1) | copy-start | bytes 1572868
  47.8 6.8 %copy-start.5 = (bf16[512,512]{1,0:T(8,128)(2,1)S(1)}, bf16[512,512]{1,0:T(8,128)(2,1)}, u32[]{:S(2)}) copy-start(bf16[512,512]{1,0:T(8,128)(2,1)} %w2_ref.1) | copy-start | bytes 1572868
  47.8 6.7 %collective-permute-start.2 = (f32[8,512]{1,0:T(8,128)S(1)}, f32[8,512]{1,0:T(8,128)S(1)}, u32[]{:S(2)}, u32[]{:S(2)}) collective-permute-start(f32[8,512]{1,0:T(8,128)S(1)} %add.10), channel_id=1, source_target_pairs={{0,2},{1,3},{2,0},{3,1},{4,6},{5,7},{6,4},{7,5},{8,10},{9,11},{10,... | collective-permute-start | bytes 49160 | tf_op jit(solution)/shard_map/ppermute | solution.py:678
  49.9 25.6 %all-to-all-start.1 = ((bf16[128,8,512]{2,1,0:T(8,128)(2,1)}), bf16[128,8,512]{2,1,0:T(8,128)(2,1)S(1)}, u32[]{:S(2)}, u32[]{:S(2)}) async-start(bf16[128,8,512]{2,1,0:T(8,128)(2,1)} %bitcast.6), calls=%async_computation.1 | async-start | bytes 2097152 | tf_op jit(solution)/shard_map/all_to_all | solution.py:669
  75.6 3.7 %collective-permute-start.3 = (f32[528,512]{1,0:T(8,128)S(1)}, f32[528,512]{1,0:T(8,128)S(1)}, u32[]{:S(2)}, u32[]{:S(2)}) collective-permute-start(f32[528,512]{1,0:T(8,128)S(1)} %get-tuple-element.45), channel_id=1, source_target_pairs={{0,4},{4,0},{1,5},{5,1},{2,6},{6,2},{3,7},{7,3},{8,12},{12,8},{9,1... | collective-permute-start | bytes 3244040 | tf_op jit(solution)/shard_map/ppermute | solution.py:674
  81.3 10.1 %copy-start.1 = (s32[512]{0:T(512)S(1)}, s32[512]{0:T(512)}, u32[]{:S(2)}) copy-start(s32[512]{0:T(512)} %param.13) | copy-start | bytes 6148
  81.3 10.1 %copy-start.2 = (s32[8]{0:T(128)S(1)}, s32[8]{0:T(128)}, u32[]{:S(2)}) copy-start(s32[8]{0:T(128)} %neg_ref.3) | copy-start | bytes 100
  81.3 10.1 %copy-start.6 = (bf16[1024,512]{1,0:T(8,128)(2,1)S(1)}, bf16[1024,512]{1,0:T(8,128)(2,1)}, u32[]{:S(2)}) copy-start(bf16[1024,512]{1,0:T(8,128)(2,1)} %get-tuple-element.50.gdst_ref) | copy-start | bytes 3145732
  81.3 23.7 %all-to-all-start.2 = ((bf16[64,8,640]{2,1,0:T(8,128)(2,1)}), bf16[64,8,640]{2,1,0:T(8,128)(2,1)S(1)}, u32[]{:S(2)}, u32[]{:S(2)}) async-start(bf16[64,8,640]{2,1,0:T(8,128)(2,1)} %bitcast.8), calls=%async_computation.2 | async-start | bytes 1310720 | tf_op jit(solution)/shard_map/all_to_all | solution.py:669
  91.4 1.2 copy-start.7
  123.6 4.9 %collective-permute-start.4 = (bf16[512,640]{1,0:T(8,128)(2,1)S(1)}, bf16[512,640]{1,0:T(8,128)(2,1)S(1)}, u32[]{:S(2)}, u32[]{:S(2)}) collective-permute-start(bf16[512,640]{1,0:T(8,128)(2,1)S(1)} %bitcast.17), channel_id=1, source_target_pairs={{0,4},{4,0},{1,5},{5,1},{2,6},{6,2},{3,7},{7,3},{8,12},{12,8},{9,1... | collective-permute-start | bytes 1966088 | tf_op jit(solution)/shard_map/ppermute | solution.py:674
